TPU v7x, 256 devices: a whole 4x4x8 slice. The times are simulated.
256 devices in a mesh: space: 16 (over z, y_hi), band: 16 (over x, y_lo, core).
Axes of the slice: x: 4, y: 4 (y_hi: 2, y_lo: 2; y = y_hi * 2 + y_lo), z: 8, core: 2. Of those that a mesh axis runs over, the one named last changes fastest.
Arguments:
- columns: float32 [64, 96, 32, 128], P('band', 'space'), may hold values from -6 to 6
- potential: float32 [96, 32, 128], P('space'), may hold values from -1 to 3
- orbitals: float32 [512, 96, 32, 128], P('band', 'space'), may hold values from -0.0390625 to 0.0390625
Outputs:
- projected: float32 [64, 96, 32, 128], P('band', 'space')
- correlation: float32 [512, 64], P('band')
All inputs are finite; a program needn't handle non-finite values.
Results may differ from a plain program's by a relative error of at most 0.00011.
Values sent between devices are 32-bit elements; how exact they have to be, the bound alone decides.
A program may use at most 64 MiB of HBM per device.

v0:
```python
import jax
import jax.numpy as jnp
from jax import lax
from jax.sharding import PartitionSpec as P

COEFFS = (
    -5369.0 / 1800.0,
    12.0 / 7.0,
    -15.0 / 56.0,
    10.0 / 189.0,
    -1.0 / 112.0,
    2.0 / 1925.0,
    -1.0 / 16632.0,
)


def padded_2(array, sides, width):
    for axis, dim in sides:
        size, length = (lax.axis_size(axis), array.shape[dim])
        up = [(i, (i + 1) % size) for i in range(size)]
        down = [(j, i) for i, j in up]
        last = lax.slice_in_dim(array, length - width, length, axis=dim)
        first = lax.slice_in_dim(array, 0, width, axis=dim)
        before = lax.ppermute(last, axis, up)
        after = lax.ppermute(first, axis, down)
        array = jnp.concatenate([before, array, after], axis=dim)
    return array


def hamiltonian(values, potential):
    padded = padded_2(values, (("space", 1),), 6)
    planes = values.shape[1]
    laplace = 3.0 * COEFFS[0] * values
    for offset in range(1, 7):
        along = (
            padded[:, 6 + offset : 6 + offset + planes]
            + padded[:, 6 - offset : 6 - offset + planes]
        )
        along = along + jnp.roll(values, offset, 2) + jnp.roll(values, -offset, 2)
        along = along + jnp.roll(values, offset, 3) + jnp.roll(values, -offset, 3)
        laplace = laplace + COEFFS[offset] * along
    return -0.5 * laplace + potential[None] * values


def shards(columns, potential, orbitals):
    applied = hamiltonian(columns, potential)
    orb_local = orbitals.shape[0]
    col_local = applied.shape[0]
    psi_flat = orbitals.reshape(orb_local, -1)
    piece = lax.all_gather(applied, "band", axis=0, tiled=True)
    partial_correlation = jnp.einsum(
        "oc,kc->ok", psi_flat, piece.reshape(piece.shape[0], -1), precision=lax.Precision.HIGHEST
    )
    correlation = lax.psum(partial_correlation, "space")
    removed = jnp.einsum("ok,oc->kc", correlation, psi_flat, precision=lax.Precision.HIGHEST)
    removed_all = lax.psum_scatter(
        removed.reshape((col_local * lax.axis_size("band"),) + applied.shape[1:]),
        "band",
        scatter_dimension=0,
        tiled=True,
    )
    projected = applied - removed_all
    return (projected, correlation)


def solution(mesh):
    placed = (
        P("band", "space", None, None),
        P("space", None, None),
        P("band", "space", None, None),
    )
    return jax.shard_map(
        shards,
        mesh=mesh,
        in_specs=placed,
        out_specs=(P("band", "space", None, None), P("band", None)),
        check_vma=False,
    )
```

profile of v0, /device:TPU:1, one launch (start us, length us, event | category | flops | bytes accessed | tf_op | source)
XLA Modules:
  0.0 268.5 jit_solution(8429235181820224546)
XLA Ops:
  7.2 0.0 copy-start
  7.2 0.0 all-gather.2.cloned.1.call-start
  7.2 3.8 %collective-permute-start.1 = (f32[4,6,32,128]{3,2,1,0:T(8,128)}, f32[4,6,32,128]{3,2,1,0:T(8,128)S(1)}, u32[]{:S(2)}, u32[]{:S(2)}) collective-permute-start(f32[4,6,32,128]{3,2,1,0:T(8,128)} %param.3), channel_id=1, source_target_pairs={{0,16},{16,32},{32,48},{48,64},{64,80},{80,96},{96,112},{112,128},... | collective-permute-start | bytes 1179656 | tf_op jit(solution)/shard_map/ppermute | solution.py:24
  11.0 5.4 %collective-permute-start = (f32[4,6,32,128]{3,2,1,0:T(8,128)}, f32[4,6,32,128]{3,2,1,0:T(8,128)S(1)}, u32[]{:S(2)}, u32[]{:S(2)}) collective-permute-start(f32[4,6,32,128]{3,2,1,0:T(8,128)} %param.3), channel_id=1, source_target_pairs={{16,0},{32,16},{48,32},{64,48},{80,64},{96,80},{112,96},{128,112},... | collective-permute-start | bytes 1179656 | tf_op jit(solution)/shard_map/ppermute | solution.py:25
  16.4 1.0 fusion.63
  17.4 1.0 fusion.59
  18.4 1.0 fusion.55
  19.3 1.0 fusion.51
  20.3 1.3 fusion.57
  21.6 0.0 copy-done
  21.6 0.1 fusion.62
  21.7 0.2 fusion.56
  21.9 0.2 fusion.53
  22.1 0.2 fusion.65
  22.3 0.2 fusion.64
  22.5 0.1 fusion.66
  22.5 0.1 fusion.58
  22.6 0.1 fusion.54
  22.7 0.2 fusion.69
  22.9 0.2 fusion.68
  23.1 0.2 fusion.52
  23.2 0.2 fusion.61
  23.4 0.1 fusion.70
  23.5 0.2 fusion.60
  23.7 0.1 fusion.50
  23.8 0.0 copy-start.3
  23.8 0.2 fusion.48
  24.0 0.2 fusion.49
  24.2 3.4 %collective-permute-done.1 = f32[4,6,32,128]{3,2,1,0:T(8,128)S(1)} collective-permute-done((f32[4,6,32,128]{3,2,1,0:T(8,128)}, f32[4,6,32,128]{3,2,1,0:T(8,128)S(1)}, u32[]{:S(2)}, u32[]{:S(2)}) %collective-permute-start.1) | collective-permute-done | bytes 393248 | tf_op jit(solution)/shard_map/ppermute | solution.py:24
  27.6 0.1 constant_dynamic-update-slice_fusion.1
  27.7 3.2 %collective-permute-done = f32[4,6,32,128]{3,2,1,0:T(8,128)S(1)} collective-permute-done((f32[4,6,32,128]{3,2,1,0:T(8,128)}, f32[4,6,32,128]{3,2,1,0:T(8,128)S(1)}, u32[]{:S(2)}, u32[]{:S(2)}) %collective-permute-start) | collective-permute-done | bytes 393248 | tf_op jit(solution)/shard_map/ppermute | solution.py:25
  30.9 0.0 copy-done.3
  30.9 0.0 copy-start.1
  30.9 3.8 %fusion.18 = f32[4,6,32,128]{3,2,1,0:T(8,128)} fusion(f32[4,12,32,128]{3,2,1,0:T(8,128)S(1)} %get-tuple-element.55, f32[4,12,32,128]{3,2,1,0:T(8,128)S(1)} %constant_dynamic-update-slice_fusion, f32[4,6,31,128]{3,2,1,0:T(8,128)S(1)} %get-tuple-element.51, f32[4,6,1,128]{3,2,1,0:T(1,128)S(1)} %get-tuple-element.53, ...), kind=kLoop, calls=%fused_computation.16 | loop fusion | flops 6881280 | bytes 15040512 | tf_op jit(solution)/shard_map/add | solution.py:42
  34.7 0.0 all-gather.2.cloned.1.call-update
  34.7 0.2 reduce-scatter.2.cloned.1.call-start
  35.0 0.0 copy-done.1
  35.0 1.8 copy.137
  36.8 2.3 copy.125
  39.1 42.7 %all-gather.2.cloned.1.call-done = f32[64,6,32,128]{3,2,1,0:T(8,128)} async-done(((f32[4,6,32,128]{3,2,1,0:T(8,128)}), f32[64,6,32,128]{3,2,1,0:T(8,128)}) %all-gather.2.cloned.1.call-update) | async-done | bytes 6291472 | tf_op jit(solution)/shard_map/all_gather | solution.py:50
  81.8 11.2 %fusion.5 = f32[32,64]{1,0:T(8,128)S(1)} fusion(f32[32,6,32,128]{3,2,1,0:T(8,128)S(1)} %copy-done.1, f32[64,6,32,128]{3,2,1,0:T(8,128)} %all-gather.2.cloned.1.call-done), kind=kOutput, calls=%fused_computation.6 | convolution fusion | flops 603979776 | bytes 9445376 | tf_op jit(solution)/shard_map/oc,kc->ok/dot_general | solution.py:51
  93.0 63.2 %psum.7 = f32[32,64]{1,0:T(8,128)S(1)} all-reduce(f32[32,64]{1,0:T(8,128)S(1)} %fusion.5), channel_id=1, replica_groups=mesh['space'=16,'band'=16] {'space'}, use_global_device_ids=true, to_apply=%region_0.1 | all-reduce | flops 2048 | bytes 16384 | tf_op jit(solution)/shard_map/psum | solution.py:54
  156.2 8.9 %fusion.2 = f32[64,6,32,128]{3,0,2,1:T(8,128)S(1)} fusion(f32[6,32,128,32]{2,1,0,3:T(8,128)} %bitcast.25, f32[32,64]{1,0:T(8,128)S(1)} %psum.7), kind=kOutput, calls=%fused_computation.3 | convolution fusion | flops 603979776 | bytes 9445376 | tf_op jit(solution)/shard_map/ok,oc->kc/dot_general | solution.py:55
  165.2 6.3 %copy.121 = f32[64,6,32,128]{3,2,1,0:T(8,128)} copy(f32[64,6,32,128]{3,0,2,1:T(8,128)S(1)} %fusion.2) | data formatting | bytes 12582912 | tf_op jit(solution)/shard_map/ok,oc->kc/dot_general | solution.py:55
  171.4 0.0 reduce-scatter.2.cloned.1.call-update
  171.5 88.4 %reduce-scatter.2.cloned.1.call-done = f32[4,6,32,128]{3,2,1,0:T(8,128)} async-done(((f32[64,6,32,128]{3,2,1,0:T(8,128)}), f32[4,6,32,128]{3,2,1,0:T(8,128)}) %reduce-scatter.2.cloned.1.call-update) | async-done | bytes 393232 | tf_op jit(solution)/shard_map/reduce_scatter | solution.py:56
  259.8 0.0 copy-done.2
  259.8 1.8 sub.3
  (7 shorter events, 0.1 us)
Async XLA Ops:
  7.2 14.5 %copy-start = (f32[4,6,32,128]{3,2,1,0:T(8,128)S(1)}, f32[4,6,32,128]{3,2,1,0:T(8,128)}, u32[]{:S(2)}) copy-start(f32[4,6,32,128]{3,2,1,0:T(8,128)} %param.3) | copy-start | bytes 1179652
  7.2 74.6 %all-gather.2.cloned.1.call-start = ((), (), s32[]{:S(2)}) async-start(), calls=%async_computation.1 | async-start | bytes 6684672 | tf_op jit(solution)/shard_map/all_gather | solution.py:50
  7.2 20.3 %collective-permute-start.1 = (f32[4,6,32,128]{3,2,1,0:T(8,128)}, f32[4,6,32,128]{3,2,1,0:T(8,128)S(1)}, u32[]{:S(2)}, u32[]{:S(2)}) collective-permute-start(f32[4,6,32,128]{3,2,1,0:T(8,128)} %param.3), channel_id=1, source_target_pairs={{0,16},{16,32},{32,48},{48,64},{64,80},{80,96},{96,112},{112,128},... | collective-permute-start | bytes 1179656 | tf_op jit(solution)/shard_map/ppermute | solution.py:24
  11.0 19.8 %collective-permute-start = (f32[4,6,32,128]{3,2,1,0:T(8,128)}, f32[4,6,32,128]{3,2,1,0:T(8,128)S(1)}, u32[]{:S(2)}, u32[]{:S(2)}) collective-permute-start(f32[4,6,32,128]{3,2,1,0:T(8,128)} %param.3), channel_id=1, source_target_pairs={{16,0},{32,16},{48,32},{64,48},{80,64},{96,80},{112,96},{128,112},... | collective-permute-start | bytes 1179656 | tf_op jit(solution)/shard_map/ppermute | solution.py:25
  23.8 7.1 %copy-start.3 = (f32[6,32,128]{2,1,0:T(8,128)S(1)}, f32[6,32,128]{2,1,0:T(8,128)}, u32[]{:S(2)}) copy-start(f32[6,32,128]{2,1,0:T(8,128)} %param.4) | copy-start | bytes 294916
  30.9 4.1 %copy-start.1 = (f32[32,6,32,128]{3,2,1,0:T(8,128)S(1)}, f32[32,6,32,128]{3,2,1,0:T(8,128)}, u32[]{:S(2)}) copy-start(f32[32,6,32,128]{3,2,1,0:T(8,128)} %param.5) | copy-start | bytes 9437188
  34.7 225.1 %reduce-scatter.2.cloned.1.call-start = ((), (), s32[]{:S(2)}) async-start(), calls=%async_computation.2 | async-start | bytes 6684672 | tf_op jit(solution)/shard_map/reduce_scatter | solution.py:56
  156.2 8.9 %copy-start.4 = (f32[32,64]{1,0:T(8,128)}, f32[32,64]{1,0:T(8,128)S(1)}, u32[]{:S(2)}) copy-start(f32[32,64]{1,0:T(8,128)S(1)} %psum.7) | copy-start | bytes 24580
  171.4 88.4 %copy-start.2 = (f32[4,6,32,128]{3,2,1,0:T(8,128)S(1)}, f32[4,6,32,128]{3,2,1,0:T(8,128)}, u32[]{:S(2)}) copy-start(f32[4,6,32,128]{3,2,1,0:T(8,128)} %fusion.18) | copy-start | bytes 1179652
Sparse Core Ops, SparseCore 0:
  34.8 46.8 all-gather.1
  171.6 88.1 reduce-scatter.1
where the time goes:
time: 270 us; the launch traced here: 268 us
  waiting for transfers between devices  138 us (51%)
  blocking collectives  63.2 us (23%)
  matrix products  20.1 us (7%)
  local copies, waits for them, and re-layouts  18.2 us (7%)
  between operations  14.2 us (5%)
  starting transfers between devices  9.46 us (4%)
  other arithmetic  5.59 us (2%)
    reduce_scatter x1, waiting for transfers between devices, shards(): lax.psum_scatter(removed.reshape((col_local * lax.axis_size('band'),) + a...  88.4 us
    psum x1, blocking collectives, shards(): correlation = lax.psum(partial_correlation, 'space')  63.2 us
    all_gather x1, waiting for transfers between devices, shards(): piece = lax.all_gather(applied, 'band', axis=0, tiled=True)  42.7 us
    dot_general x1, matrix products, shards(): jnp.einsum('oc,kc->ok', psi_flat, piece.reshape(piece.shape[0], -1), prec...  11.2 us
    dot_general x1, matrix products, shards(): jnp.einsum('ok,oc->kc', correlation, psi_flat, precision=lax.Precision.HI...  8.91 us
    dot_general x1, local copies, waits for them, and re-layouts, shards(): jnp.einsum('ok,oc->kc', correlation, psi_flat, precision=lax.Precision.HI...  6.27 us
  transfers between devices with their start and end apart: 4, of which 4 were waited for; matrix products, arithmetic and copies ran while one was open for 4% of the time, Pallas kernels for 0%

commit v1 on v0

v1 whole, which is shorter than its diff:
```python
import jax
import jax.numpy as jnp
from jax import lax
from jax.experimental import pallas as pl
from jax.experimental.pallas import tpu as pltpu
from jax.sharding import PartitionSpec as P

COEFFS = (
    -5369.0 / 1800.0,
    12.0 / 7.0,
    -15.0 / 56.0,
    10.0 / 189.0,
    -1.0 / 112.0,
    2.0 / 1925.0,
    -1.0 / 16632.0,
)

MESH = pl.DeviceIdType.MESH
NZ_RING, NX_RING = 8, 4
COLS, ORBS = 4, 32
PLANES, NY, NX = 6, 32, 128
ROWS = PLANES * NY
PART = ROWS // 8

STEPS = ((0, 0), (0, 1), (1, 0), (1, 1), (3, 0), (3, 1), (2, 0), (2, 1))


def kernel(
    col_hbm, pot_ref, orb_hbm, proj_ref, corr_ref,
    colv, halo, app, phibuf, phi, acol, ahl, cpart, cin, zin, ctot, cts,
    rsend, rrecv, rown, fin, rem,
    loc_sem, orb_s, orb_r, halo_s, halo_r, col_s, col_r, fwd_s, fwd_r,
    s1_s, s1_r, s2_s, s2_r, s3_s, s3_r, ry_s, ry_r, fin_s, fin_r,
):
    s, b = lax.axis_index("space"), lax.axis_index("band")
    z, h = s // 2, s % 2
    x, yl, c = b // 4, (b // 2) % 2, b % 2
    me = x * 2 + c

    def dev(dz=0, dh=0, dx=0, dy=0, dc=0):
        return (
            ((z + dz) % NZ_RING) * 2 + (h + dh) % 2,
            ((x + dx) % NX_RING) * 4 + ((yl + dy) % 2) * 2 + (c + dc) % 2,
        )

    def part_of(dx, dc):
        return ((x + dx) % NX_RING) * 2 + (c + dc) % 2

    def rows_of(g):
        return pl.ds(pl.multiple_of(g * PART, PART), PART)

    def slot_of(side, g):
        return pl.ds((side * 8 + g) * COLS, COLS)

    after, before = ((s + 1) % 16, b), ((s + 15) % 16, b)
    partner = dev(dy=1)

    barrier = pltpu.get_barrier_semaphore()
    peers = [dev(dx=dx, dc=dc, dh=dh) for dh in (0, 1) for dx, dc in STEPS if (dx, dc, dh) != (0, 0, 0)]
    peers += [dev(dz=dz) for dz in range(1, NZ_RING)]
    far_slab = (((s + 15) % 16) * (1 - h) + ((s + 1) % 16) * h, b)
    peers += [partner, far_slab]
    for peer in peers:
        pl.semaphore_signal(barrier, inc=1, device_id=peer, device_id_type=MESH)

    load_col = pltpu.make_async_copy(col_hbm, colv, loc_sem.at[0])
    load_col.start()
    load_orb = pltpu.make_async_copy(orb_hbm.at[:, rows_of(me), :], phibuf.at[pl.ds(0, ORBS)], loc_sem.at[1])
    load_orb.start()

    pl.semaphore_wait(barrier, len(peers))

    halos = [
        pltpu.make_async_remote_copy(
            col_hbm, halo.at[i], halo_s.at[i], halo_r.at[i], device_id=to, device_id_type=MESH
        )
        for i, to in ((0, after), (1, before))
    ]
    for copy in halos:
        copy.start()
    orbs = {}
    for i, (dx, dc) in enumerate(STEPS):
        if i > 0:
            orbs[i] = pltpu.make_async_remote_copy(
                orb_hbm.at[:, rows_of(part_of(dx, dc)), :],
                phibuf.at[pl.ds(i * ORBS, ORBS)],
                orb_s.at[i],
                orb_r.at[i],
                device_id=dev(dx=dx, dc=dc),
                device_id_type=MESH,
            )
    for i in (1, 2, 4, 3, 5, 6):
        orbs[i].start()

    load_col.wait()

    def local_terms(j, carry):
        planes = [colv[j, pl.ds(p * NY, NY), :] for p in range(PLANES)]
        for p in range(PLANES):
            v = planes[p]
            total = (pot_ref[pl.ds(p * NY, NY), :] - 1.5 * COEFFS[0]) * v
            for k in range(1, 7):
                along = pltpu.roll(v, k, 0) + pltpu.roll(v, NY - k, 0)
                along = along + (pltpu.roll(v, k, 1) + pltpu.roll(v, NX - k, 1))
                if p - k >= 0:
                    along = along + planes[p - k]
                if p + k < PLANES:
                    along = along + planes[p + k]
                total = total + (-0.5 * COEFFS[k]) * along
            app[j, pl.ds(p * NY, NY), :] = total
        return carry

    lax.fori_loop(0, COLS, local_terms, 0)

    def lay_out(i0, n):
        def one(q, carry):
            value = phibuf[pl.ds(i0 * ORBS, n * ORBS), q, :]
            high = value.astype(jnp.bfloat16)
            low = (value - high.astype(jnp.float32)).astype(jnp.bfloat16)
            at = pl.ds(pl.multiple_of(q * NX, NX), NX)
            phi[0, pl.ds(i0 * ORBS, n * ORBS), at] = high
            phi[1, pl.ds(i0 * ORBS, n * ORBS), at] = low
            return carry

        lax.fori_loop(0, PART, one, 0)

    load_orb.wait()
    orbs[1].wait_recv()
    lay_out(0, 2)

    for copy in halos:
        copy.wait_recv()

    def halo_terms(j, carry):
        for p in range(PLANES):
            total = app[j, pl.ds(p * NY, NY), :]
            for k in range(1, 7):
                if p - k < 0:
                    total = total + (-0.5 * COEFFS[k]) * halo[0, j, pl.ds((p - k + PLANES) * NY, NY), :]
                if p + k >= PLANES:
                    total = total + (-0.5 * COEFFS[k]) * halo[1, j, pl.ds((p + k - PLANES) * NY, NY), :]
            app[j, pl.ds(p * NY, NY), :] = total
        return carry

    lax.fori_loop(0, COLS, halo_terms, 0)

    own_col = pltpu.make_async_copy(app.at[:, rows_of(me), :], acol.at[slot_of(yl, me)], loc_sem.at[2])
    own_col.start()
    cols, fwds = {}, {}
    for i, (dx, dc) in enumerate(STEPS):
        if i > 0:
            cols[i] = pltpu.make_async_remote_copy(
                app.at[:, rows_of(part_of(dx, dc)), :],
                acol.at[slot_of(yl, me)],
                col_s.at[i],
                col_r.at[i],
                device_id=dev(dx=dx, dc=dc),
                device_id_type=MESH,
            )
        came = slot_of(yl, part_of(-dx, -dc))
        fwds[i] = pltpu.make_async_remote_copy(
            app.at[:, rows_of(me), :] if i == 0 else acol.at[came],
            acol.at[came],
            fwd_s.at[i],
            fwd_r.at[i],
            device_id=partner,
            device_id_type=MESH,
        )
    for i in (6, 7, 2, 4, 3, 5, 1):
        cols[i].start()
    fwds[0].start()
    orbs[7].start()
    for i in (1, 2, 4, 3, 5, 6, 7):
        cols[i].wait_recv()
        fwds[i].start()

    for i in (2, 3, 4, 5):
        orbs[i].wait_recv()
    lay_out(2, 4)

    own_col.wait()
    for i in range(8):
        fwds[i].wait_recv()

    def lay_out_columns(q, carry):
        value = acol[:, q, :]
        high = value.astype(jnp.bfloat16)
        low = (value - high.astype(jnp.float32)).astype(jnp.bfloat16)
        at = pl.ds(pl.multiple_of(q * NX, NX), NX)
        ahl[pl.ds(0, 64), at] = high
        ahl[pl.ds(64, 64), at] = low
        return carry

    lax.fori_loop(0, PART, lay_out_columns, 0)

    half_lanes = lax.broadcasted_iota(jnp.int32, (16, 128), 1) < 64
    dims = (((1,), (1,)), ((), ()))

    def correlate(i0, n):
        rows = pl.ds(i0 * ORBS, n * ORBS)
        high = lax.dot_general(phi[0, rows, :], ahl[...], dims, preferred_element_type=jnp.float32)
        low = lax.dot_general(phi[1, rows, :], ahl[...], dims, preferred_element_type=jnp.float32)
        value = high + pltpu.roll(high, 64, 1) + low
        for i in range(n):
            first = value[i * ORBS : i * ORBS + 16]
            second = value[i * ORBS + 16 : i * ORBS + 32]
            packed = jnp.where(half_lanes, first, pltpu.roll(second, 64, 1))
            cpart[i0 + i, 0] = packed[:8]
            cpart[i0 + i, 1] = packed[8:]

    sums = {}

    def send_parts(i):
        dx, dc = STEPS[i]
        for dh in (0, 1):
            if (i, dh) != (0, 0):
                n = i * 2 + dh
                sums[n] = pltpu.make_async_remote_copy(
                    cpart.at[i, (h + dh) % 2],
                    cin.at[n],
                    s1_s.at[n],
                    s1_r.at[n],
                    device_id=dev(dx=-dx, dc=-dc, dh=dh),
                    device_id_type=MESH,
                )
                sums[n].start()

    correlate(0, 6)
    for i in (2, 4, 3, 5, 1, 0):
        send_parts(i)
    for i in (6, 7):
        orbs[i].wait_recv()
    lay_out(6, 2)
    correlate(6, 2)
    send_parts(6)
    send_parts(7)

    total = cpart[0, h]
    for n in range(1, 16):
        sums[n].wait_recv()
        total = total + cin[n]

    zin[z] = total
    zs = []
    for dz in (4, 3, 5, 2, 6, 1, 7):
        copy = pltpu.make_async_remote_copy(
            zin.at[z], zin.at[z], s2_s.at[dz], s2_r.at[dz], device_id=dev(dz=dz), device_id_type=MESH
        )
        copy.start()
        zs.append(copy)
    for copy in zs:
        copy.wait_recv()
    total = zin[0]
    for n in range(1, NZ_RING):
        total = total + zin[n]

    ctot[0, h] = total
    backs = []
    for i in (6, 7, 2, 4, 3, 5, 1, 0):
        dx, dc = STEPS[i]
        for dh in (1, 0):
            if (i, dh) != (0, 0):
                n = i * 2 + dh
                copy = pltpu.make_async_remote_copy(
                    ctot.at[0, h],
                    ctot.at[i, h],
                    s3_s.at[n],
                    s3_r.at[n],
                    device_id=dev(dx=dx, dc=dc, dh=dh),
                    device_id_type=MESH,
                )
                copy.start()
                backs.append(copy)
    for copy in backs:
        copy.wait_recv()

    packed = ctot[...].reshape(8, 16, 128)
    swapped = pltpu.roll(packed.reshape(128, 128), 64, 1).reshape(8, 16, 128)
    corr = jnp.concatenate([packed, swapped], axis=1).reshape(256, 128)
    flat = jnp.transpose(corr)[:64]
    high = flat.astype(jnp.bfloat16)
    low = (flat - high.astype(jnp.float32)).astype(jnp.bfloat16)
    for side in (0, 1):
        cts[side, pl.ds(0, 32), :] = high[side * 32 : side * 32 + 32]
        cts[side, pl.ds(32, 32), :] = low[side * 32 : side * 32 + 32]

    def removed(side, out):
        for q0 in range(0, PART, 4):
            at = pl.ds(q0 * NX, 4 * NX)
            both = jnp.dot(cts[side], phi[0, :, at], preferred_element_type=jnp.float32)
            rest = jnp.dot(cts[side, pl.ds(0, 32), :], phi[1, :, at], preferred_element_type=jnp.float32)
            value = both[:32] + both[32:] + rest
            for q in range(4):
                for k in range(NX_RING):
                    out[k, q0 + q] = value[k * 8 : k * 8 + 8, q * NX : (q + 1) * NX]

    removed(1 - yl, rsend)
    order = (2, 1, 3, 0)
    ys = {}
    for dx in order:
        k = (x + dx) % NX_RING
        ys[dx] = pltpu.make_async_remote_copy(
            rsend.at[k], rrecv.at[k], ry_s.at[dx], ry_r.at[dx], device_id=partner, device_id_type=MESH
        )
        ys[dx].start()
    removed(yl, rown)

    own = corr[:32]
    lane = lax.broadcasted_iota(jnp.int32, (ORBS, 128), 1)
    value = own
    for side in (0, 1):
        for k in range(NX_RING):
            source, target = side * 32 + k * 8, k * 16 + side * 8
            if source != target:
                moved = pltpu.roll(own, (target - source) % 128, 1)
                value = jnp.where((lane >= target) & (lane < target + 8), moved, value)
    corr_ref[...] = value[:, :64]

    fins = {}
    for dx in order:
        k = (x + dx) % NX_RING
        ys[dx].wait_recv()
        for j in range(8):
            fin[k, j] = rown[k, :, j, :] + rrecv[k, :, j, :]
        for dc in (1, 0):
            source = fin.at[k, pl.ds(((c + dc) % 2) * COLS, COLS)]
            target = rem.at[:, rows_of(me), :]
            n = STEPS.index((dx, dc))
            if n == 0:
                local = pltpu.make_async_copy(source, target, loc_sem.at[3])
                local.start()
            else:
                fins[n] = pltpu.make_async_remote_copy(
                    source, target, fin_s.at[n], fin_r.at[n], device_id=dev(dx=dx, dc=dc), device_id_type=MESH
                )
                fins[n].start()
    local.wait()
    for copy in fins.values():
        copy.wait_recv()
    proj_ref[...] = app[...] - rem[...]

    for group in (halos, orbs.values(), cols.values(), fwds.values(), sums.values(), zs, backs, ys.values(), fins.values()):
        for copy in group:
            copy.wait_send()


def shards(columns, potential, orbitals):
    f32, bf16 = jnp.float32, jnp.bfloat16
    dma = pltpu.SemaphoreType.DMA
    scratch = [
        pltpu.VMEM((COLS, ROWS, NX), f32),
        pltpu.VMEM((2, COLS, ROWS, NX), f32),
        pltpu.VMEM((COLS, ROWS, NX), f32),
        pltpu.VMEM((8 * ORBS, PART, NX), f32),
        pltpu.VMEM((2, 8 * ORBS, PART * NX), bf16),
        pltpu.VMEM((64, PART, NX), f32),
        pltpu.VMEM((128, PART * NX), bf16),
        pltpu.VMEM((8, 2, 8, 128), f32),
        pltpu.VMEM((16, 8, 128), f32),
        pltpu.VMEM((NZ_RING, 8, 128), f32),
        pltpu.VMEM((8, 2, 8, 128), f32),
        pltpu.VMEM((2, 64, 256), bf16),
        pltpu.VMEM((NX_RING, PART, 8, NX), f32),
        pltpu.VMEM((NX_RING, PART, 8, NX), f32),
        pltpu.VMEM((NX_RING, PART, 8, NX), f32),
        pltpu.VMEM((NX_RING, 8, PART, NX), f32),
        pltpu.VMEM((COLS, ROWS, NX), f32),
        dma((4,)),
        dma((8,)), dma((8,)),
        dma((2,)), dma((2,)),
        dma((8,)), dma((8,)),
        dma((8,)), dma((8,)),
        dma((16,)), dma((16,)),
        dma((8,)), dma((8,)),
        dma((16,)), dma((16,)),
        dma((4,)), dma((4,)),
        dma((8,)), dma((8,)),
    ]
    vmem, anywhere = pl.BlockSpec(memory_space=pltpu.VMEM), pl.BlockSpec(memory_space=pl.ANY)
    projected, correlation = pl.pallas_call(
        kernel,
        out_shape=(
            jax.ShapeDtypeStruct((COLS, ROWS, NX), f32),
            jax.ShapeDtypeStruct((ORBS, 64), f32),
        ),
        in_specs=[anywhere, vmem, anywhere],
        out_specs=(vmem, vmem),
        scratch_shapes=scratch,
        compiler_params=pltpu.CompilerParams(
            collective_id=0, has_side_effects=True, vmem_limit_bytes=40 * 2**20
        ),
        name="sternheimer",
    )(
        columns.reshape(COLS, ROWS, NX),
        potential.reshape(ROWS, NX),
        orbitals.reshape(ORBS, ROWS, NX),
    )
    return projected.reshape(columns.shape), correlation


def solution(mesh):
    placed = (
        P("band", "space", None, None),
        P("space", None, None),
        P("band", "space", None, None),
    )
    return jax.shard_map(
        shards,
        mesh=mesh,
        in_specs=placed,
        out_specs=(P("band", "space", None, None), P("band", None)),
        check_vma=False,
    )
```

time: 270 us -> 89.6 us (0.33)
  waiting for transfers between devices: 138 us -> 0 us
  Pallas kernels: 0 us -> 83.7 us
  blocking collectives: 63.2 us -> 0 us
  matrix products: 20.1 us -> 0 us
  between operations: 14.2 us -> 0.65 us
  local copies, waits for them, and re-layouts: 18.2 us -> 5.12 us
  starting transfers between devices: 9.46 us -> 0 us
  other arithmetic: 5.59 us -> 0 us
    reduce_scatter x1 -> x0, waiting for transfers between devices: 88.4 us -> none  [shards(): lax.psum_scatter(removed.reshape((col_local * lax.axis_size('band'),) + a...]
    pallas_call x0 -> x1, Pallas kernels: none -> 83.7 us  [shards(): pl.pallas_call(kernel, out_shape=(jax.ShapeDtypeStruct((COLS, ROWS, NX),...]
    psum x1 -> x0, blocking collectives: 63.2 us -> none  [shards(): correlation = lax.psum(partial_correlation, 'space')]
    all_gather x1 -> x0, waiting for transfers between devices: 42.7 us -> none  [shards(): piece = lax.all_gather(applied, 'band', axis=0, tiled=True)]
    dot_general x2 -> x0, matrix products: 20.1 us -> none  [the longest x1 11.2 us: shards(): jnp.einsum('oc,kc->ok', psi_flat, piece.reshape(piece.shape[0], -1), prec...]
    ppermute x2 -> x0, starting transfers between devices: 9.2 us -> none  [the longest x1 5.38 us: padded_2(): after = lax.ppermute(first, axis, down)]
    slice x24 -> x0, local copies, waits for them, and re-layouts: 7.68 us -> none  [the longest x12 4.31 us: hamiltonian(): along = along + jnp.roll(values, offset, 2) + jnp.roll(values, -offset, 2)]
    ppermute x2 -> x0, waiting for transfers between devices: 6.52 us -> none  [the longest x1 3.36 us: padded_2(): before = lax.ppermute(last, axis, up)]
  transfers between devices with their start and end apart: 4 -> 0, of which waited for: 4 -> 0; matrix products, arithmetic and copies ran while one was open for 4% -> 0% of each run, Pallas kernels for 0% -> 0%
where the time goes in v1:
time: 89.6 us; the launch traced here: 89.4 us
  Pallas kernels  83.7 us (93%)
  local copies, waits for them, and re-layouts  5.12 us (6%)
    pallas_call x1, Pallas kernels, shards(): pl.pallas_call(kernel, out_shape=(jax.ShapeDtypeStruct((COLS, ROWS, NX),...  83.7 us
    unnamed x8, local copies, waits for them, and re-layouts  5.12 us

profile of v1, /device:TPU:1, one launch (start us, length us, event | category | flops | bytes accessed | tf_op | source)
XLA Modules:
  0.0 89.4 jit_solution(2625899339920292864)
XLA Ops:
  0.6 0.0 copy-start
  0.6 1.9 %copy-done = f32[32,6,32,128]{3,2,1,0:T(8,128)S(1)} copy-done((f32[32,6,32,128]{3,2,1,0:T(8,128)S(1)}, f32[32,6,32,128]{3,2,1,0:T(8,128)}, u32[]{:S(2)}) %copy-start) | copy-done | bytes 3145752
  2.5 0.0 copy-start.1
  2.5 1.0 %copy-done.1 = f32[4,6,32,128]{3,2,1,0:T(8,128)S(1)} copy-done((f32[4,6,32,128]{3,2,1,0:T(8,128)S(1)}, f32[4,6,32,128]{3,2,1,0:T(8,128)}, u32[]{:S(2)}) %copy-start.1) | copy-done | bytes 393240
  3.5 0.0 copy-start.2
  3.5 0.9 copy-done.2
  4.4 83.7 %sternheimer.1 = (f32[4,192,128]{2,1,0:T(8,128)S(1)}, f32[32,64]{1,0:T(8,128)S(1)}) custom-call(f32[4,192,128]{2,1,0:T(8,128)S(1)} %bitcast.5, f32[192,128]{1,0:T(8,128)S(1)} %bitcast.7, f32[32,192,128]{2,1,0:T(8,128)S(1)} %bitcast.4), custom_call_target="tpu_custom_call" | custom-call | tf_op jit(solution)/shard_map/sternheimer/pallas_call | solution.py:380
  88.1 0.7 copy.7
  88.8 0.6 copy.8
Async XLA Ops:
  0.6 1.9 %copy-start = (f32[32,6,32,128]{3,2,1,0:T(8,128)S(1)}, f32[32,6,32,128]{3,2,1,0:T(8,128)}, u32[]{:S(2)}) copy-start(f32[32,6,32,128]{3,2,1,0:T(8,128)} %param.5) | copy-start | bytes 9437188
  2.5 1.0 %copy-start.1 = (f32[4,6,32,128]{3,2,1,0:T(8,128)S(1)}, f32[4,6,32,128]{3,2,1,0:T(8,128)}, u32[]{:S(2)}) copy-start(f32[4,6,32,128]{3,2,1,0:T(8,128)} %param.3) | copy-start | bytes 1179652
  3.5 0.9 copy-start.2

commit v2 on v1

--- a/solution.py
+++ b/solution.py
@@ -26,10 +26,10 @@
 
 
 def kernel(
-    col_hbm, pot_ref, orb_hbm, proj_ref, corr_ref,
-    colv, halo, app, phibuf, phi, acol, ahl, cpart, cin, zin, ctot, cts,
+    col_hbm, pot_hbm, orb_hbm, proj_ref, corr_ref,
+    colv, potv, relay, halo, app, phibuf, phi, acol, ahl, cpart, cin, zin, ctot, cts,
     rsend, rrecv, rown, fin, rem,
-    loc_sem, orb_s, orb_r, halo_s, halo_r, col_s, col_r, fwd_s, fwd_r,
+    loc_sem, near_sem, orb_s, orb_r, h1_s, h1_r, h2_s, h2_r, h3_s, h3_r, col_s, col_r, fwd_s, fwd_r,
     s1_s, s1_r, s2_s, s2_r, s3_s, s3_r, ry_s, ry_r, fin_s, fin_r,
 ):
     s, b = lax.axis_index("space"), lax.axis_index("band")
@@ -52,32 +52,58 @@
     def slot_of(side, g):
         return pl.ds((side * 8 + g) * COLS, COLS)
 
-    after, before = ((s + 1) % 16, b), ((s + 15) % 16, b)
+    def along_y(step):
+        y = (h * 2 + yl + step + 4) % 4
+        return y // 2, (z * 2 + y // 2, x * 4 + (y % 2) * 2 + c)
+
+    def signal(sem, to):
+        pl.semaphore_signal(sem, inc=1, device_id=to, device_id_type=MESH)
+
     partner = dev(dy=1)
 
     barrier = pltpu.get_barrier_semaphore()
-    peers = [dev(dx=dx, dc=dc, dh=dh) for dh in (0, 1) for dx, dc in STEPS if (dx, dc, dh) != (0, 0, 0)]
-    peers += [dev(dz=dz) for dz in range(1, NZ_RING)]
-    far_slab = (((s + 15) % 16) * (1 - h) + ((s + 1) % 16) * h, b)
-    peers += [partner, far_slab]
+    peers = [dev(dx=dx, dc=dc) for dx, dc in STEPS[1:]]
+    peers += [along_y(1)[1], along_y(-1)[1], dev(dz=1), dev(dz=NZ_RING - 1)]
     for peer in peers:
-        pl.semaphore_signal(barrier, inc=1, device_id=peer, device_id_type=MESH)
+        signal(barrier, peer)
 
     load_col = pltpu.make_async_copy(col_hbm, colv, loc_sem.at[0])
     load_col.start()
+    load_pot = pltpu.make_async_copy(pot_hbm, potv, loc_sem.at[4])
+    load_pot.start()
     load_orb = pltpu.make_async_copy(orb_hbm.at[:, rows_of(me), :], phibuf.at[pl.ds(0, ORBS)], loc_sem.at[1])
     load_orb.start()
 
     pl.semaphore_wait(barrier, len(peers))
 
-    halos = [
-        pltpu.make_async_remote_copy(
-            col_hbm, halo.at[i], halo_s.at[i], halo_r.at[i], device_id=to, device_id_type=MESH
-        )
-        for i, to in ((0, after), (1, before))
-    ]
-    for copy in halos:
-        copy.start()
+    signal(near_sem.at[0], dev(dz=1))
+    signal(near_sem.at[1], dev(dz=NZ_RING - 1))
+    hop1, hop2, hop3 = [], [], []
+    for j in (0, 2, 1, 3):
+        step = 1 if j < 2 else -1
+        h_to, to = along_y(step)
+        hop1.append(
+            pltpu.make_async_remote_copy(
+                col_hbm.at[j], relay.at[j], h1_s.at[j], h1_r.at[j], device_id=to, device_id_type=MESH
+            )
+        )
+        hop2.append(
+            pltpu.make_async_remote_copy(
+                relay.at[j], halo.at[1 - h_to, j], h2_s.at[j], h2_r.at[j], device_id=to, device_id_type=MESH
+            )
+        )
+        hop3.append(
+            pltpu.make_async_remote_copy(
+                halo.at[1 - h, j],
+                halo.at[h, j],
+                h3_s.at[j],
+                h3_r.at[j],
+                device_id=(((z + 1 - 2 * h + NZ_RING) % NZ_RING) * 2 + h, b),
+                device_id_type=MESH,
+            )
+        )
+        hop1[-1].start()
+
     orbs = {}
     for i, (dx, dc) in enumerate(STEPS):
         if i > 0:
@@ -89,16 +115,17 @@
                 device_id=dev(dx=dx, dc=dc),
                 device_id_type=MESH,
             )
-    for i in (1, 2, 4, 3, 5, 6):
+    for i in (1, 2, 4, 3, 5):
         orbs[i].start()
 
     load_col.wait()
+    load_pot.wait()
 
     def local_terms(j, carry):
         planes = [colv[j, pl.ds(p * NY, NY), :] for p in range(PLANES)]
         for p in range(PLANES):
             v = planes[p]
-            total = (pot_ref[pl.ds(p * NY, NY), :] - 1.5 * COEFFS[0]) * v
+            total = (potv[pl.ds(p * NY, NY), :] - 1.5 * COEFFS[0]) * v
             for k in range(1, 7):
                 along = pltpu.roll(v, k, 0) + pltpu.roll(v, NY - k, 0)
                 along = along + (pltpu.roll(v, k, 1) + pltpu.roll(v, NX - k, 1))
@@ -112,23 +139,45 @@
 
     lax.fori_loop(0, COLS, local_terms, 0)
 
-    def lay_out(i0, n):
-        def one(q, carry):
-            value = phibuf[pl.ds(i0 * ORBS, n * ORBS), q, :]
-            high = value.astype(jnp.bfloat16)
-            low = (value - high.astype(jnp.float32)).astype(jnp.bfloat16)
-            at = pl.ds(pl.multiple_of(q * NX, NX), NX)
-            phi[0, pl.ds(i0 * ORBS, n * ORBS), at] = high
-            phi[1, pl.ds(i0 * ORBS, n * ORBS), at] = low
+    def split(value):
+        high = value.astype(jnp.bfloat16)
+        return high, (value - high.astype(jnp.float32)).astype(jnp.bfloat16)
+
+    def lay_out(ref, store, r0, blocks):
+        def one(r, carry):
+            rows = pl.ds(pl.multiple_of(r0 + r * 16, 16), 16)
+            for q0 in range(0, PART, 8):
+                high, low = split(jnp.swapaxes(ref[rows, q0 : q0 + 8, :], 0, 1))
+                for q in range(8):
+                    store(r0 + r * 16, pl.ds((q0 + q) * NX, NX), high[q], low[q])
             return carry
 
-        lax.fori_loop(0, PART, one, 0)
-
+        lax.fori_loop(0, blocks, one, 0)
+
+    def store_orbitals(row, at, high, low):
+        rows = pl.ds(pl.multiple_of(row, 16), 16)
+        phi[0, rows, at] = high
+        phi[1, rows, at] = low
+
+    def store_columns(row, at, high, low):
+        ahl[pl.ds(pl.multiple_of(row, 16), 16), at] = high
+        ahl[pl.ds(pl.multiple_of(64 + row, 16), 16), at] = low
+
+    for copy, onward in zip(hop1, hop2):
+        copy.wait_recv()
+        onward.start()
     load_orb.wait()
     orbs[1].wait_recv()
-    lay_out(0, 2)
-
-    for copy in halos:
+    lay_out(phibuf, store_orbitals, 0, 4)
+    for copy, onward in zip(hop2, hop3):
+        copy.wait_recv()
+        onward.start()
+    for i in (0, 1):
+        pl.semaphore_wait(near_sem.at[i], 1)
+    signal(near_sem.at[2], dev(dz=2))
+    signal(near_sem.at[3], dev(dz=NZ_RING - 2))
+
+    for copy in hop3:
         copy.wait_recv()
 
     def halo_terms(j, carry):
@@ -169,6 +218,7 @@
     for i in (6, 7, 2, 4, 3, 5, 1):
         cols[i].start()
     fwds[0].start()
+    orbs[6].start()
     orbs[7].start()
     for i in (1, 2, 4, 3, 5, 6, 7):
         cols[i].wait_recv()
@@ -176,22 +226,13 @@
 
     for i in (2, 3, 4, 5):
         orbs[i].wait_recv()
-    lay_out(2, 4)
+    lay_out(phibuf, store_orbitals, 64, 8)
 
     own_col.wait()
     for i in range(8):
         fwds[i].wait_recv()
 
-    def lay_out_columns(q, carry):
-        value = acol[:, q, :]
-        high = value.astype(jnp.bfloat16)
-        low = (value - high.astype(jnp.float32)).astype(jnp.bfloat16)
-        at = pl.ds(pl.multiple_of(q * NX, NX), NX)
-        ahl[pl.ds(0, 64), at] = high
-        ahl[pl.ds(64, 64), at] = low
-        return carry
-
-    lax.fori_loop(0, PART, lay_out_columns, 0)
+    lay_out(acol, store_columns, 0, 4)
 
     half_lanes = lax.broadcasted_iota(jnp.int32, (16, 128), 1) < 64
     dims = (((1,), (1,)), ((), ()))
@@ -230,7 +271,7 @@
         send_parts(i)
     for i in (6, 7):
         orbs[i].wait_recv()
-    lay_out(6, 2)
+    lay_out(phibuf, store_orbitals, 192, 4)
     correlate(6, 2)
     send_parts(6)
     send_parts(7)
@@ -241,6 +282,8 @@
         total = total + cin[n]
 
     zin[z] = total
+    for i in (2, 3):
+        pl.semaphore_wait(near_sem.at[i], 1)
     zs = []
     for dz in (4, 3, 5, 2, 6, 1, 7):
         copy = pltpu.make_async_remote_copy(
@@ -278,8 +321,7 @@
     swapped = pltpu.roll(packed.reshape(128, 128), 64, 1).reshape(8, 16, 128)
     corr = jnp.concatenate([packed, swapped], axis=1).reshape(256, 128)
     flat = jnp.transpose(corr)[:64]
-    high = flat.astype(jnp.bfloat16)
-    low = (flat - high.astype(jnp.float32)).astype(jnp.bfloat16)
+    high, low = split(flat)
     for side in (0, 1):
         cts[side, pl.ds(0, 32), :] = high[side * 32 : side * 32 + 32]
         cts[side, pl.ds(32, 32), :] = low[side * 32 : side * 32 + 32]
@@ -320,8 +362,7 @@
     for dx in order:
         k = (x + dx) % NX_RING
         ys[dx].wait_recv()
-        for j in range(8):
-            fin[k, j] = rown[k, :, j, :] + rrecv[k, :, j, :]
+        fin[k] = jnp.swapaxes(rown[k] + rrecv[k], 0, 1)
         for dc in (1, 0):
             source = fin.at[k, pl.ds(((c + dc) % 2) * COLS, COLS)]
             target = rem.at[:, rows_of(me), :]
@@ -339,7 +380,7 @@
         copy.wait_recv()
     proj_ref[...] = app[...] - rem[...]
 
-    for group in (halos, orbs.values(), cols.values(), fwds.values(), sums.values(), zs, backs, ys.values(), fins.values()):
+    for group in (hop1, hop2, hop3, orbs.values(), cols.values(), fwds.values(), sums.values(), zs, backs, ys.values(), fins.values()):
         for copy in group:
             copy.wait_send()
 
@@ -348,6 +389,8 @@
     f32, bf16 = jnp.float32, jnp.bfloat16
     dma = pltpu.SemaphoreType.DMA
     scratch = [
+        pltpu.VMEM((COLS, ROWS, NX), f32),
+        pltpu.VMEM((ROWS, NX), f32),
         pltpu.VMEM((COLS, ROWS, NX), f32),
         pltpu.VMEM((2, COLS, ROWS, NX), f32),
         pltpu.VMEM((COLS, ROWS, NX), f32),
@@ -365,9 +408,10 @@
         pltpu.VMEM((NX_RING, PART, 8, NX), f32),
         pltpu.VMEM((NX_RING, 8, PART, NX), f32),
         pltpu.VMEM((COLS, ROWS, NX), f32),
-        dma((4,)),
+        dma((5,)),
+        pltpu.SemaphoreType.REGULAR((4,)),
         dma((8,)), dma((8,)),
-        dma((2,)), dma((2,)),
+        dma((4,)), dma((4,)), dma((4,)), dma((4,)), dma((4,)), dma((4,)),
         dma((8,)), dma((8,)),
         dma((8,)), dma((8,)),
         dma((16,)), dma((16,)),
@@ -383,11 +427,11 @@
             jax.ShapeDtypeStruct((COLS, ROWS, NX), f32),
             jax.ShapeDtypeStruct((ORBS, 64), f32),
         ),
-        in_specs=[anywhere, vmem, anywhere],
+        in_specs=[anywhere, anywhere, anywhere],
         out_specs=(vmem, vmem),
         scratch_shapes=scratch,
         compiler_params=pltpu.CompilerParams(
-            collective_id=0, has_side_effects=True, vmem_limit_bytes=40 * 2**20
+            collective_id=0, has_side_effects=True, vmem_limit_bytes=60 * 2**20
         ),
         name="sternheimer",
     )(

time: 89.6 us -> 82.9 us (0.925)
  Pallas kernels: 83.7 us -> 79 us
  local copies, waits for them, and re-layouts: 5.12 us -> 3.09 us
    pallas_call x1, Pallas kernels: 83.7 us -> 79 us  [shards(): pl.pallas_call(kernel, out_shape=(jax.ShapeDtypeStruct((COLS, ROWS, NX),...]
    unnamed x8 -> x2, local copies, waits for them, and re-layouts: 5.12 us -> 3.09 us
where the time goes in v2:
time: 82.9 us; the launch traced here: 82.7 us
  Pallas kernels  79 us (95%)
  local copies, waits for them, and re-layouts  3.09 us (4%)
    pallas_call x1, Pallas kernels, shards(): pl.pallas_call(kernel, out_shape=(jax.ShapeDtypeStruct((COLS, ROWS, NX),...  79 us
    unnamed x2, local copies, waits for them, and re-layouts  3.09 us

profile of v2, /device:TPU:1, one launch (start us, length us, event | category | flops | bytes accessed | tf_op | source)
XLA Modules:
  0.0 82.7 jit_solution(9492199665274228682)
XLA Ops:
  0.6 79.0 %sternheimer.1 = (f32[4,192,128]{2,1,0:T(8,128)}, f32[32,64]{1,0:T(8,128)}) custom-call(f32[4,192,128]{2,1,0:T(8,128)} %bitcast.5, f32[192,128]{1,0:T(8,128)} %bitcast.7, f32[32,192,128]{2,1,0:T(8,128)} %bitcast.4), custom_call_target="tpu_custom_call" | custom-call | tf_op jit(solution)/shard_map/sternheimer/pallas_call | solution.py:424
  79.6 1.8 %copy.7 = f32[4,6,32,128]{3,2,1,0:T(8,128)} copy(f32[4,6,32,128]{3,2,1,0:T(8,128)} %bitcast.6) | data formatting | bytes 786432
  81.4 1.3 %copy.8 = f32[32,64]{1,0:T(8,128)} copy(f32[32,64]{1,0:T(8,128)} %get-tuple-element.9) | data formatting | bytes 16384

commit v3 on v2

--- a/solution.py
+++ b/solution.py
@@ -20,17 +20,20 @@
 COLS, ORBS = 4, 32
 PLANES, NY, NX = 6, 32, 128
 ROWS = PLANES * NY
-PART = ROWS // 8
+PART = 16
+SPLIT = 8 * PART
 
 STEPS = ((0, 0), (0, 1), (1, 0), (1, 1), (3, 0), (3, 1), (2, 0), (2, 1))
+STEPS_Y = ((0, 0), (0, 1), (1, 0), (1, 1))
 
 
 def kernel(
     col_hbm, pot_hbm, orb_hbm, proj_ref, corr_ref,
-    colv, potv, relay, halo, app, phibuf, phi, acol, ahl, cpart, cin, zin, ctot, cts,
-    rsend, rrecv, rown, fin, rem,
+    colv, potv, relay, halo, app, phibuf, phi, acol, ahl, cpart, cin, zin, ctot, cts, cts_y,
+    rsend, rrecv, rown, fin, ry, ryin, fin_y, rem,
     loc_sem, near_sem, orb_s, orb_r, h1_s, h1_r, h2_s, h2_r, h3_s, h3_r, col_s, col_r, fwd_s, fwd_r,
-    s1_s, s1_r, s2_s, s2_r, s3_s, s3_r, ry_s, ry_r, fin_s, fin_r,
+    orby_s, orby_r, coly_s, coly_r, gat_s, gat_r,
+    s1_s, s1_r, s2_s, s2_r, s3_s, s3_r, ry_s, ry_r, fin_s, fin_r, rx_s, rx_r, finy_s, finy_r,
 ):
     s, b = lax.axis_index("space"), lax.axis_index("band")
     z, h = s // 2, s % 2
@@ -49,6 +52,10 @@
     def rows_of(g):
         return pl.ds(pl.multiple_of(g * PART, PART), PART)
 
+    def rows_y(dy, dc):
+        g = ((yl + dy) % 2) * 2 + (c + dc) % 2
+        return pl.ds(pl.multiple_of(SPLIT + g * PART, PART), PART)
+
     def slot_of(side, g):
         return pl.ds((side * 8 + g) * COLS, COLS)
 
@@ -63,7 +70,7 @@
 
     barrier = pltpu.get_barrier_semaphore()
     peers = [dev(dx=dx, dc=dc) for dx, dc in STEPS[1:]]
-    peers += [along_y(1)[1], along_y(-1)[1], dev(dz=1), dev(dz=NZ_RING - 1)]
+    peers += [along_y(1)[1], along_y(-1)[1], dev(dy=1, dc=1), dev(dz=1), dev(dz=NZ_RING - 1)]
     for peer in peers:
         signal(barrier, peer)
 
@@ -73,6 +80,8 @@
     load_pot.start()
     load_orb = pltpu.make_async_copy(orb_hbm.at[:, rows_of(me), :], phibuf.at[pl.ds(0, ORBS)], loc_sem.at[1])
     load_orb.start()
+    load_orb_y = pltpu.make_async_copy(orb_hbm.at[:, rows_y(0, 0), :], phibuf.at[pl.ds(8 * ORBS, ORBS)], loc_sem.at[5])
+    load_orb_y.start()
 
     pl.semaphore_wait(barrier, len(peers))
 
@@ -115,8 +124,21 @@
                 device_id=dev(dx=dx, dc=dc),
                 device_id_type=MESH,
             )
-    for i in (1, 2, 4, 3, 5):
+    orbs_y = {}
+    for i, (dy, dc) in enumerate(STEPS_Y):
+        if i > 0:
+            orbs_y[i] = pltpu.make_async_remote_copy(
+                orb_hbm.at[:, rows_y(dy, dc), :],
+                phibuf.at[pl.ds((8 + i) * ORBS, ORBS)],
+                orby_s.at[i],
+                orby_r.at[i],
+                device_id=dev(dy=dy, dc=dc),
+                device_id_type=MESH,
+            )
+    for i in (2, 4, 3, 5, 1):
         orbs[i].start()
+    orbs_y[1].start()
+    orbs[6].start()
 
     load_col.wait()
     load_pot.wait()
@@ -159,9 +181,12 @@
         phi[0, rows, at] = high
         phi[1, rows, at] = low
 
-    def store_columns(row, at, high, low):
-        ahl[pl.ds(pl.multiple_of(row, 16), 16), at] = high
-        ahl[pl.ds(pl.multiple_of(64 + row, 16), 16), at] = low
+    def columns_to(mode):
+        def store(row, at, high, low):
+            ahl[mode, pl.ds(pl.multiple_of(row, 16), 16), at] = high
+            ahl[mode, pl.ds(pl.multiple_of(64 + row, 16), 16), at] = low
+
+        return store
 
     for copy, onward in zip(hop1, hop2):
         copy.wait_recv()
@@ -169,9 +194,14 @@
     load_orb.wait()
     orbs[1].wait_recv()
     lay_out(phibuf, store_orbitals, 0, 4)
+    load_orb_y.wait()
+    orbs_y[1].wait_recv()
+    lay_out(phibuf, store_orbitals, 256, 4)
     for copy, onward in zip(hop2, hop3):
         copy.wait_recv()
         onward.start()
+    orbs_y[2].start()
+    orbs_y[3].start()
     for i in (0, 1):
         pl.semaphore_wait(near_sem.at[i], 1)
     signal(near_sem.at[2], dev(dz=2))
@@ -193,14 +223,16 @@
 
     lax.fori_loop(0, COLS, halo_terms, 0)
 
-    own_col = pltpu.make_async_copy(app.at[:, rows_of(me), :], acol.at[slot_of(yl, me)], loc_sem.at[2])
+    own_col = pltpu.make_async_copy(app.at[:, rows_of(me), :], acol.at[0, slot_of(yl, me)], loc_sem.at[2])
     own_col.start()
-    cols, fwds = {}, {}
+    own_col_y = pltpu.make_async_copy(app.at[:, rows_y(0, 0), :], acol.at[1, slot_of(yl, me)], loc_sem.at[6])
+    own_col_y.start()
+    cols, fwds, cols_y, gathers = {}, {}, {}, {}
     for i, (dx, dc) in enumerate(STEPS):
         if i > 0:
             cols[i] = pltpu.make_async_remote_copy(
                 app.at[:, rows_of(part_of(dx, dc)), :],
-                acol.at[slot_of(yl, me)],
+                acol.at[0, slot_of(yl, me)],
                 col_s.at[i],
                 col_r.at[i],
                 device_id=dev(dx=dx, dc=dc),
@@ -208,76 +240,121 @@
             )
         came = slot_of(yl, part_of(-dx, -dc))
         fwds[i] = pltpu.make_async_remote_copy(
-            app.at[:, rows_of(me), :] if i == 0 else acol.at[came],
-            acol.at[came],
+            app.at[:, rows_of(me), :] if i == 0 else acol.at[0, came],
+            acol.at[0, came],
             fwd_s.at[i],
             fwd_r.at[i],
             device_id=partner,
             device_id_type=MESH,
         )
+    for i, (dy, dc) in enumerate(STEPS_Y):
+        if i > 0:
+            cols_y[i] = pltpu.make_async_remote_copy(
+                app.at[:, rows_y(dy, dc), :],
+                acol.at[1, slot_of(yl, me)],
+                coly_s.at[i],
+                coly_r.at[i],
+                device_id=dev(dy=dy, dc=dc),
+                device_id_type=MESH,
+            )
+    for dx in (2, 1, 3):
+        for dy in (0, 1):
+            block = acol.at[1, pl.ds(((yl + dy) % 2) * 32 + x * 8, 8)]
+            gathers[dx * 2 + dy] = pltpu.make_async_remote_copy(
+                block, block, gat_s.at[dx * 2 + dy], gat_r.at[dx * 2 + dy], device_id=dev(dx=dx), device_id_type=MESH
+            )
     for i in (6, 7, 2, 4, 3, 5, 1):
         cols[i].start()
+    for i in (2, 3, 1):
+        cols_y[i].start()
     fwds[0].start()
-    orbs[6].start()
     orbs[7].start()
-    for i in (1, 2, 4, 3, 5, 6, 7):
+    own_col_y.wait()
+    cols_y[1].wait_recv()
+    for dx in (2, 1, 3):
+        gathers[dx * 2].start()
+    for i in (1, 2, 4, 3, 5):
+        cols[i].wait_recv()
+        fwds[i].start()
+    for i in (2, 3):
+        cols_y[i].wait_recv()
+    for dx in (2, 1, 3):
+        gathers[dx * 2 + 1].start()
+    for i in (6, 7):
         cols[i].wait_recv()
         fwds[i].start()
 
     for i in (2, 3, 4, 5):
         orbs[i].wait_recv()
     lay_out(phibuf, store_orbitals, 64, 8)
+    for i in (2, 3):
+        orbs_y[i].wait_recv()
+    lay_out(phibuf, store_orbitals, 320, 4)
 
     own_col.wait()
     for i in range(8):
         fwds[i].wait_recv()
-
-    lay_out(acol, store_columns, 0, 4)
+    lay_out(acol.at[0], columns_to(0), 0, 4)
 
     half_lanes = lax.broadcasted_iota(jnp.int32, (16, 128), 1) < 64
     dims = (((1,), (1,)), ((), ()))
 
-    def correlate(i0, n):
+    def correlate(mode, i0, n):
         rows = pl.ds(i0 * ORBS, n * ORBS)
-        high = lax.dot_general(phi[0, rows, :], ahl[...], dims, preferred_element_type=jnp.float32)
-        low = lax.dot_general(phi[1, rows, :], ahl[...], dims, preferred_element_type=jnp.float32)
+        high = lax.dot_general(phi[0, rows, :], ahl[mode], dims, preferred_element_type=jnp.float32)
+        low = lax.dot_general(phi[1, rows, :], ahl[mode], dims, preferred_element_type=jnp.float32)
         value = high + pltpu.roll(high, 64, 1) + low
         for i in range(n):
             first = value[i * ORBS : i * ORBS + 16]
             second = value[i * ORBS + 16 : i * ORBS + 32]
             packed = jnp.where(half_lanes, first, pltpu.roll(second, 64, 1))
-            cpart[i0 + i, 0] = packed[:8]
-            cpart[i0 + i, 1] = packed[8:]
+            if i0 + i in (8, 9):
+                cpart[i0 + i - 8, 0] += packed[:8]
+                cpart[i0 + i - 8, 1] += packed[8:]
+            else:
+                cpart[i0 + i, 0] = packed[:8]
+                cpart[i0 + i, 1] = packed[8:]
 
     sums = {}
 
     def send_parts(i):
-        dx, dc = STEPS[i]
+        if i < 8:
+            dx, dc = STEPS[i]
+            dy, n0 = 0, i * 2
+        else:
+            dx, (dy, dc) = 0, STEPS_Y[i - 8]
+            n0 = i * 2 - 4
         for dh in (0, 1):
             if (i, dh) != (0, 0):
-                n = i * 2 + dh
+                n = n0 + dh
                 sums[n] = pltpu.make_async_remote_copy(
                     cpart.at[i, (h + dh) % 2],
                     cin.at[n],
                     s1_s.at[n],
                     s1_r.at[n],
-                    device_id=dev(dx=-dx, dc=-dc, dh=dh),
+                    device_id=dev(dx=-dx, dy=dy, dc=-dc, dh=dh),
                     device_id_type=MESH,
                 )
                 sums[n].start()
 
-    correlate(0, 6)
-    for i in (2, 4, 3, 5, 1, 0):
+    correlate(0, 0, 6)
+    for i in (2, 4, 3, 5):
+        send_parts(i)
+    for copy in gathers.values():
+        copy.wait_recv()
+    lay_out(acol.at[1], columns_to(1), 0, 4)
+    correlate(1, 8, 4)
+    for i in (10, 11, 1, 0):
         send_parts(i)
     for i in (6, 7):
         orbs[i].wait_recv()
     lay_out(phibuf, store_orbitals, 192, 4)
-    correlate(6, 2)
+    correlate(0, 6, 2)
     send_parts(6)
     send_parts(7)
 
     total = cpart[0, h]
-    for n in range(1, 16):
+    for n in range(1, 20):
         sums[n].wait_recv()
         total = total + cin[n]
 
@@ -299,8 +376,10 @@
 
     ctot[0, h] = total
     backs = []
-    for i in (6, 7, 2, 4, 3, 5, 1, 0):
-        dx, dc = STEPS[i]
+    users = [(i, dx, 0, dc) for i, (dx, dc) in enumerate(STEPS)]
+    users += [(8, 0, 1, 0), (9, 0, 1, 1)]
+    for i in (6, 7, 8, 9, 2, 4, 3, 5, 1, 0):
+        _, dx, dy, dc = users[i]
         for dh in (1, 0):
             if (i, dh) != (0, 0):
                 n = i * 2 + dh
@@ -309,7 +388,7 @@
                     ctot.at[i, h],
                     s3_s.at[n],
                     s3_r.at[n],
-                    device_id=dev(dx=dx, dc=dc, dh=dh),
+                    device_id=dev(dx=dx, dy=dy, dc=dc, dh=dh),
                     device_id_type=MESH,
                 )
                 copy.start()
@@ -317,26 +396,37 @@
     for copy in backs:
         copy.wait_recv()
 
-    packed = ctot[...].reshape(8, 16, 128)
-    swapped = pltpu.roll(packed.reshape(128, 128), 64, 1).reshape(8, 16, 128)
-    corr = jnp.concatenate([packed, swapped], axis=1).reshape(256, 128)
-    flat = jnp.transpose(corr)[:64]
-    high, low = split(flat)
-    for side in (0, 1):
-        cts[side, pl.ds(0, 32), :] = high[side * 32 : side * 32 + 32]
-        cts[side, pl.ds(32, 32), :] = low[side * 32 : side * 32 + 32]
-
-    def removed(side, out):
+    packed = ctot[...].reshape(10, 16, 128)
+    swapped = pltpu.roll(packed.reshape(160, 128), 64, 1).reshape(10, 16, 128)
+    corr = jnp.concatenate([packed, swapped], axis=1).reshape(320, 128)
+    corr_y = jnp.concatenate([corr[:64], corr[256:]], axis=0)
+
+    def operands(value, out):
+        high, low = split(jnp.transpose(value)[:64])
+        for side in (0, 1):
+            out[side, pl.ds(0, 32), :] = high[side * 32 : side * 32 + 32]
+            out[side, pl.ds(32, 32), :] = low[side * 32 : side * 32 + 32]
+
+    operands(corr[:256], cts)
+
+    def removed(left, rows, side, out):
         for q0 in range(0, PART, 4):
             at = pl.ds(q0 * NX, 4 * NX)
-            both = jnp.dot(cts[side], phi[0, :, at], preferred_element_type=jnp.float32)
-            rest = jnp.dot(cts[side, pl.ds(0, 32), :], phi[1, :, at], preferred_element_type=jnp.float32)
+            both = jnp.dot(left[side], phi[0, rows, at], preferred_element_type=jnp.float32)
+            rest = jnp.dot(left[side, pl.ds(0, 32), :], phi[1, rows, at], preferred_element_type=jnp.float32)
             value = both[:32] + both[32:] + rest
             for q in range(4):
                 for k in range(NX_RING):
-                    out[k, q0 + q] = value[k * 8 : k * 8 + 8, q * NX : (q + 1) * NX]
-
-    removed(1 - yl, rsend)
+                    out(k, q0 + q, value[k * 8 : k * 8 + 8, q * NX : (q + 1) * NX])
+
+    def to_send(k, q, value):
+        rsend[k, q] = value
+
+    def to_own(k, q, value):
+        rown[k, q] = value
+
+    first, last = pl.ds(0, 256), pl.ds(256, 128)
+    removed(cts, first, 1 - yl, to_send)
     order = (2, 1, 3, 0)
     ys = {}
     for dx in order:
@@ -345,7 +435,20 @@
             rsend.at[k], rrecv.at[k], ry_s.at[dx], ry_r.at[dx], device_id=partner, device_id_type=MESH
         )
         ys[dx].start()
-    removed(yl, rown)
+    operands(corr_y, cts_y)
+    for side in (0, 1):
+
+        def to_x(k, q, value):
+            ry[k, side, q] = value
+
+        removed(cts_y, last, side, to_x)
+    xs = {}
+    for dx in (2, 1, 3):
+        xs[dx] = pltpu.make_async_remote_copy(
+            ry.at[(x + dx) % NX_RING], ryin.at[dx], rx_s.at[dx], rx_r.at[dx], device_id=dev(dx=dx), device_id_type=MESH
+        )
+        xs[dx].start()
+    removed(cts, first, yl, to_own)
 
     own = corr[:32]
     lane = lax.broadcasted_iota(jnp.int32, (ORBS, 128), 1)
@@ -375,12 +478,33 @@
                     source, target, fin_s.at[n], fin_r.at[n], device_id=dev(dx=dx, dc=dc), device_id_type=MESH
                 )
                 fins[n].start()
+    value = ry[x]
+    for dx in (1, 3, 2):
+        xs[dx].wait_recv()
+        value = value + ryin[dx]
+    for side in (0, 1):
+        fin_y[side] = jnp.swapaxes(value[side], 0, 1)
+    for i in (2, 3, 1, 0):
+        dy, dc = STEPS_Y[i]
+        source = fin_y.at[(yl + dy) % 2, pl.ds(((c + dc) % 2) * COLS, COLS)]
+        target = rem.at[:, rows_y(0, 0), :]
+        if i == 0:
+            local_y = pltpu.make_async_copy(source, target, loc_sem.at[7])
+            local_y.start()
+        else:
+            fins[8 + i] = pltpu.make_async_remote_copy(
+                source, target, finy_s.at[i], finy_r.at[i], device_id=dev(dy=dy, dc=dc), device_id_type=MESH
+            )
+            fins[8 + i].start()
     local.wait()
+    local_y.wait()
     for copy in fins.values():
         copy.wait_recv()
     proj_ref[...] = app[...] - rem[...]
 
-    for group in (hop1, hop2, hop3, orbs.values(), cols.values(), fwds.values(), sums.values(), zs, backs, ys.values(), fins.values()):
+    groups = [hop1, hop2, hop3, zs, backs]
+    groups += [g.values() for g in (orbs, orbs_y, cols, fwds, cols_y, gathers, sums, ys, xs, fins)]
+    for group in groups:
         for copy in group:
             copy.wait_send()
 
@@ -394,31 +518,40 @@
         pltpu.VMEM((COLS, ROWS, NX), f32),
         pltpu.VMEM((2, COLS, ROWS, NX), f32),
         pltpu.VMEM((COLS, ROWS, NX), f32),
-        pltpu.VMEM((8 * ORBS, PART, NX), f32),
-        pltpu.VMEM((2, 8 * ORBS, PART * NX), bf16),
-        pltpu.VMEM((64, PART, NX), f32),
-        pltpu.VMEM((128, PART * NX), bf16),
-        pltpu.VMEM((8, 2, 8, 128), f32),
-        pltpu.VMEM((16, 8, 128), f32),
+        pltpu.VMEM((12 * ORBS, PART, NX), f32),
+        pltpu.VMEM((2, 12 * ORBS, PART * NX), bf16),
+        pltpu.VMEM((2, 64, PART, NX), f32),
+        pltpu.VMEM((2, 128, PART * NX), bf16),
+        pltpu.VMEM((12, 2, 8, 128), f32),
+        pltpu.VMEM((20, 8, 128), f32),
         pltpu.VMEM((NZ_RING, 8, 128), f32),
-        pltpu.VMEM((8, 2, 8, 128), f32),
+        pltpu.VMEM((10, 2, 8, 128), f32),
         pltpu.VMEM((2, 64, 256), bf16),
+        pltpu.VMEM((2, 64, 128), bf16),
         pltpu.VMEM((NX_RING, PART, 8, NX), f32),
         pltpu.VMEM((NX_RING, PART, 8, NX), f32),
         pltpu.VMEM((NX_RING, PART, 8, NX), f32),
         pltpu.VMEM((NX_RING, 8, PART, NX), f32),
+        pltpu.VMEM((NX_RING, 2, PART, 8, NX), f32),
+        pltpu.VMEM((NX_RING, 2, PART, 8, NX), f32),
+        pltpu.VMEM((2, 8, PART, NX), f32),
         pltpu.VMEM((COLS, ROWS, NX), f32),
-        dma((5,)),
+        dma((8,)),
         pltpu.SemaphoreType.REGULAR((4,)),
         dma((8,)), dma((8,)),
         dma((4,)), dma((4,)), dma((4,)), dma((4,)), dma((4,)), dma((4,)),
         dma((8,)), dma((8,)),
         dma((8,)), dma((8,)),
-        dma((16,)), dma((16,)),
-        dma((8,)), dma((8,)),
-        dma((16,)), dma((16,)),
+        dma((4,)), dma((4,)),
         dma((4,)), dma((4,)),
         dma((8,)), dma((8,)),
+        dma((20,)), dma((20,)),
+        dma((8,)), dma((8,)),
+        dma((20,)), dma((20,)),
+        dma((4,)), dma((4,)),
+        dma((8,)), dma((8,)),
+        dma((4,)), dma((4,)),
+        dma((4,)), dma((4,)),
     ]
     vmem, anywhere = pl.BlockSpec(memory_space=pltpu.VMEM), pl.BlockSpec(memory_space=pl.ANY)
     projected, correlation = pl.pallas_call(

time: 82.9 us -> 78.5 us (0.947)
  Pallas kernels: 79 us -> 74.6 us
    pallas_call x1, Pallas kernels: 79 us -> 74.6 us  [shards(): pl.pallas_call(kernel, out_shape=(jax.ShapeDtypeStruct((COLS, ROWS, NX),...]
where the time goes in v3:
time: 78.5 us; the launch traced here: 78.3 us
  Pallas kernels  74.6 us (95%)
  local copies, waits for them, and re-layouts  3.09 us (4%)
    pallas_call x1, Pallas kernels, shards(): pl.pallas_call(kernel, out_shape=(jax.ShapeDtypeStruct((COLS, ROWS, NX),...  74.6 us
    unnamed x2, local copies, waits for them, and re-layouts  3.09 us

profile of v3, /device:TPU:1, one launch (start us, length us, event | category | flops | bytes accessed | tf_op | source)
XLA Modules:
  0.0 78.3 jit_solution(536549158839854857)
XLA Ops:
  0.6 74.6 %sternheimer.1 = (f32[4,192,128]{2,1,0:T(8,128)}, f32[32,64]{1,0:T(8,128)}) custom-call(f32[4,192,128]{2,1,0:T(8,128)} %bitcast.5, f32[192,128]{1,0:T(8,128)} %bitcast.7, f32[32,192,128]{2,1,0:T(8,128)} %bitcast.4), custom_call_target="tpu_custom_call" | custom-call | tf_op jit(solution)/shard_map/sternheimer/pallas_call | solution.py:557
  75.3 1.8 %copy.7 = f32[4,6,32,128]{3,2,1,0:T(8,128)} copy(f32[4,6,32,128]{3,2,1,0:T(8,128)} %bitcast.6) | data formatting | bytes 786432
  77.0 1.3 %copy.8 = f32[32,64]{1,0:T(8,128)} copy(f32[32,64]{1,0:T(8,128)} %get-tuple-element.9) | data formatting | bytes 16384

commit v4 on v3

--- a/solution.py
+++ b/solution.py
@@ -29,9 +29,9 @@
 
 def kernel(
     col_hbm, pot_hbm, orb_hbm, proj_ref, corr_ref,
-    colv, potv, relay, halo, app, phibuf, phi, acol, ahl, cpart, cin, zin, ctot, cts, cts_y,
+    colv, potv, halo, app, phibuf, phi, acol, ahl, cpart, cin, zin, ctot, cts, cts_y,
     rsend, rrecv, rown, fin, ry, ryin, fin_y, rem,
-    loc_sem, near_sem, orb_s, orb_r, h1_s, h1_r, h2_s, h2_r, h3_s, h3_r, col_s, col_r, fwd_s, fwd_r,
+    loc_sem, near_sem, orb_s, orb_r, h_s, h_r, col_s, col_r, fwd_s, fwd_r,
     orby_s, orby_r, coly_s, coly_r, gat_s, gat_r,
     s1_s, s1_r, s2_s, s2_r, s3_s, s3_r, ry_s, ry_r, fin_s, fin_r, rx_s, rx_r, finy_s, finy_r,
 ):
@@ -59,18 +59,15 @@
     def slot_of(side, g):
         return pl.ds((side * 8 + g) * COLS, COLS)
 
-    def along_y(step):
-        y = (h * 2 + yl + step + 4) % 4
-        return y // 2, (z * 2 + y // 2, x * 4 + (y % 2) * 2 + c)
-
     def signal(sem, to):
         pl.semaphore_signal(sem, inc=1, device_id=to, device_id_type=MESH)
 
     partner = dev(dy=1)
+    same_z, other_z = dev(dh=1), (((s + 16 + 2 * h - 1) % 16), b)
 
     barrier = pltpu.get_barrier_semaphore()
     peers = [dev(dx=dx, dc=dc) for dx, dc in STEPS[1:]]
-    peers += [along_y(1)[1], along_y(-1)[1], dev(dy=1, dc=1), dev(dz=1), dev(dz=NZ_RING - 1)]
+    peers += [partner, dev(dy=1, dc=1), same_z, other_z, dev(dz=1), dev(dz=NZ_RING - 1)]
     for peer in peers:
         signal(barrier, peer)
 
@@ -87,31 +84,18 @@
 
     signal(near_sem.at[0], dev(dz=1))
     signal(near_sem.at[1], dev(dz=NZ_RING - 1))
-    hop1, hop2, hop3 = [], [], []
-    for j in (0, 2, 1, 3):
-        step = 1 if j < 2 else -1
-        h_to, to = along_y(step)
-        hop1.append(
-            pltpu.make_async_remote_copy(
-                col_hbm.at[j], relay.at[j], h1_s.at[j], h1_r.at[j], device_id=to, device_id_type=MESH
-            )
+
+    def halo_copy(j, source, side, sem, to):
+        return pltpu.make_async_remote_copy(
+            source, halo.at[side, j], h_s.at[sem], h_r.at[sem], device_id=to, device_id_type=MESH
         )
-        hop2.append(
-            pltpu.make_async_remote_copy(
-                relay.at[j], halo.at[1 - h_to, j], h2_s.at[j], h2_r.at[j], device_id=to, device_id_type=MESH
-            )
-        )
-        hop3.append(
-            pltpu.make_async_remote_copy(
-                halo.at[1 - h, j],
-                halo.at[h, j],
-                h3_s.at[j],
-                h3_r.at[j],
-                device_id=(((z + 1 - 2 * h + NZ_RING) % NZ_RING) * 2 + h, b),
-                device_id_type=MESH,
-            )
-        )
-        hop1[-1].start()
+
+    to_same = [halo_copy(j, col_hbm.at[j], h, j, same_z) for j in range(COLS)]
+    to_other = [halo_copy(j, col_hbm.at[j], 1 - h, 4 + j, other_z) for j in range(2)]
+    beside = ((z + 1 - 2 * h + NZ_RING) % NZ_RING) * 2 + h, b
+    onward = [halo_copy(j, halo.at[1 - h, j], h, 4 + j, beside) for j in range(2, COLS)]
+    for copy in (to_same[2], to_same[3], to_other[0], to_same[0], to_other[1], to_same[1]):
+        copy.start()
 
     orbs = {}
     for i, (dx, dc) in enumerate(STEPS):
@@ -160,6 +144,9 @@
         return carry
 
     lax.fori_loop(0, COLS, local_terms, 0)
+    for copy, follower in zip(to_same[2:], onward):
+        copy.wait_recv()
+        follower.start()
 
     def split(value):
         high = value.astype(jnp.bfloat16)
@@ -188,26 +175,20 @@
 
         return store
 
-    for copy, onward in zip(hop1, hop2):
-        copy.wait_recv()
-        onward.start()
+    orbs_y[2].start()
+    orbs_y[3].start()
     load_orb.wait()
     orbs[1].wait_recv()
     lay_out(phibuf, store_orbitals, 0, 4)
     load_orb_y.wait()
     orbs_y[1].wait_recv()
     lay_out(phibuf, store_orbitals, 256, 4)
-    for copy, onward in zip(hop2, hop3):
-        copy.wait_recv()
-        onward.start()
-    orbs_y[2].start()
-    orbs_y[3].start()
     for i in (0, 1):
         pl.semaphore_wait(near_sem.at[i], 1)
     signal(near_sem.at[2], dev(dz=2))
     signal(near_sem.at[3], dev(dz=NZ_RING - 2))
 
-    for copy in hop3:
+    for copy in (*onward, *to_same[:2], *to_other):
         copy.wait_recv()
 
     def halo_terms(j, carry):
@@ -284,9 +265,9 @@
         cols[i].wait_recv()
         fwds[i].start()
 
-    for i in (2, 3, 4, 5):
+    for i in (2, 3, 4, 5, 6, 7):
         orbs[i].wait_recv()
-    lay_out(phibuf, store_orbitals, 64, 8)
+    lay_out(phibuf, store_orbitals, 64, 12)
     for i in (2, 3):
         orbs_y[i].wait_recv()
     lay_out(phibuf, store_orbitals, 320, 4)
@@ -337,8 +318,8 @@
                 )
                 sums[n].start()
 
-    correlate(0, 0, 6)
-    for i in (2, 4, 3, 5):
+    correlate(0, 0, 8)
+    for i in (6, 7, 2, 4, 3, 5):
         send_parts(i)
     for copy in gathers.values():
         copy.wait_recv()
@@ -346,12 +327,6 @@
     correlate(1, 8, 4)
     for i in (10, 11, 1, 0):
         send_parts(i)
-    for i in (6, 7):
-        orbs[i].wait_recv()
-    lay_out(phibuf, store_orbitals, 192, 4)
-    correlate(0, 6, 2)
-    send_parts(6)
-    send_parts(7)
 
     total = cpart[0, h]
     for n in range(1, 20):
@@ -407,8 +382,6 @@
             out[side, pl.ds(0, 32), :] = high[side * 32 : side * 32 + 32]
             out[side, pl.ds(32, 32), :] = low[side * 32 : side * 32 + 32]
 
-    operands(corr[:256], cts)
-
     def removed(left, rows, side, out):
         for q0 in range(0, PART, 4):
             at = pl.ds(q0 * NX, 4 * NX)
@@ -426,6 +399,20 @@
         rown[k, q] = value
 
     first, last = pl.ds(0, 256), pl.ds(256, 128)
+    operands(corr_y, cts_y)
+    for side in (0, 1):
+
+        def to_x(k, q, value):
+            ry[k, side, q] = value
+
+        removed(cts_y, last, side, to_x)
+    xs = {}
+    for dx in (2, 1, 3):
+        xs[dx] = pltpu.make_async_remote_copy(
+            ry.at[(x + dx) % NX_RING], ryin.at[dx], rx_s.at[dx], rx_r.at[dx], device_id=dev(dx=dx), device_id_type=MESH
+        )
+        xs[dx].start()
+    operands(corr[:256], cts)
     removed(cts, first, 1 - yl, to_send)
     order = (2, 1, 3, 0)
     ys = {}
@@ -435,19 +422,6 @@
             rsend.at[k], rrecv.at[k], ry_s.at[dx], ry_r.at[dx], device_id=partner, device_id_type=MESH
         )
         ys[dx].start()
-    operands(corr_y, cts_y)
-    for side in (0, 1):
-
-        def to_x(k, q, value):
-            ry[k, side, q] = value
-
-        removed(cts_y, last, side, to_x)
-    xs = {}
-    for dx in (2, 1, 3):
-        xs[dx] = pltpu.make_async_remote_copy(
-            ry.at[(x + dx) % NX_RING], ryin.at[dx], rx_s.at[dx], rx_r.at[dx], device_id=dev(dx=dx), device_id_type=MESH
-        )
-        xs[dx].start()
     removed(cts, first, yl, to_own)
 
     own = corr[:32]
@@ -502,7 +476,7 @@
         copy.wait_recv()
     proj_ref[...] = app[...] - rem[...]
 
-    groups = [hop1, hop2, hop3, zs, backs]
+    groups = [to_same, to_other, onward, zs, backs]
     groups += [g.values() for g in (orbs, orbs_y, cols, fwds, cols_y, gathers, sums, ys, xs, fins)]
     for group in groups:
         for copy in group:
@@ -515,7 +489,6 @@
     scratch = [
         pltpu.VMEM((COLS, ROWS, NX), f32),
         pltpu.VMEM((ROWS, NX), f32),
-        pltpu.VMEM((COLS, ROWS, NX), f32),
         pltpu.VMEM((2, COLS, ROWS, NX), f32),
         pltpu.VMEM((COLS, ROWS, NX), f32),
         pltpu.VMEM((12 * ORBS, PART, NX), f32),
@@ -539,7 +512,7 @@
         dma((8,)),
         pltpu.SemaphoreType.REGULAR((4,)),
         dma((8,)), dma((8,)),
-        dma((4,)), dma((4,)), dma((4,)), dma((4,)), dma((4,)), dma((4,)),
+        dma((8,)), dma((8,)),
         dma((8,)), dma((8,)),
         dma((8,)), dma((8,)),
         dma((4,)), dma((4,)),

time: 78.5 us -> 77.1 us (0.982)
  Pallas kernels: 74.6 us -> 73.2 us
    pallas_call x1, Pallas kernels: 74.6 us -> 73.2 us  [shards(): pl.pallas_call(kernel, out_shape=(jax.ShapeDtypeStruct((COLS, ROWS, NX),...]
where the time goes in v4:
time: 77.1 us; the launch traced here: 76.9 us
  Pallas kernels  73.2 us (95%)
  local copies, waits for them, and re-layouts  3.09 us (4%)
    pallas_call x1, Pallas kernels, shards(): pl.pallas_call(kernel, out_shape=(jax.ShapeDtypeStruct((COLS, ROWS, NX),...  73.2 us
    unnamed x2, local copies, waits for them, and re-layouts  3.09 us

profile of v4, /device:TPU:1, one launch (start us, length us, event | category | flops | bytes accessed | tf_op | source)
XLA Modules:
  0.0 76.9 jit_solution(323814372001321335)
XLA Ops:
  0.6 73.2 %sternheimer.1 = (f32[4,192,128]{2,1,0:T(8,128)}, f32[32,64]{1,0:T(8,128)}) custom-call(f32[4,192,128]{2,1,0:T(8,128)} %bitcast.5, f32[192,128]{1,0:T(8,128)} %bitcast.7, f32[32,192,128]{2,1,0:T(8,128)} %bitcast.4), custom_call_target="tpu_custom_call" | custom-call | tf_op jit(solution)/shard_map/sternheimer/pallas_call | solution.py:530
  73.8 1.8 %copy.7 = f32[4,6,32,128]{3,2,1,0:T(8,128)} copy(f32[4,6,32,128]{3,2,1,0:T(8,128)} %bitcast.6) | data formatting | bytes 786432
  75.6 1.3 %copy.8 = f32[32,64]{1,0:T(8,128)} copy(f32[32,64]{1,0:T(8,128)} %get-tuple-element.9) | data formatting | bytes 16384

commit v5 on v4

--- a/solution.py
+++ b/solution.py
@@ -30,7 +30,7 @@
 def kernel(
     col_hbm, pot_hbm, orb_hbm, proj_ref, corr_ref,
     colv, potv, halo, app, phibuf, phi, acol, ahl, cpart, cin, zin, ctot, cts, cts_y,
-    rsend, rrecv, rown, fin, ry, ryin, fin_y, rem,
+    rsend, rrecv, rown, fin, ry, ryin, rysum, fin_y, rem,
     loc_sem, near_sem, orb_s, orb_r, h_s, h_r, col_s, col_r, fwd_s, fwd_r,
     orby_s, orby_r, coly_s, coly_r, gat_s, gat_r,
     s1_s, s1_r, s2_s, s2_r, s3_s, s3_r, ry_s, ry_r, fin_s, fin_r, rx_s, rx_r, finy_s, finy_r,
@@ -63,11 +63,11 @@
         pl.semaphore_signal(sem, inc=1, device_id=to, device_id_type=MESH)
 
     partner = dev(dy=1)
-    same_z, other_z = dev(dh=1), (((s + 16 + 2 * h - 1) % 16), b)
+    same_z = dev(dh=1)
 
     barrier = pltpu.get_barrier_semaphore()
     peers = [dev(dx=dx, dc=dc) for dx, dc in STEPS[1:]]
-    peers += [partner, dev(dy=1, dc=1), same_z, other_z, dev(dz=1), dev(dz=NZ_RING - 1)]
+    peers += [partner, dev(dy=1, dc=1), same_z, dev(dz=1), dev(dz=NZ_RING - 1)]
     for peer in peers:
         signal(barrier, peer)
 
@@ -85,16 +85,25 @@
     signal(near_sem.at[0], dev(dz=1))
     signal(near_sem.at[1], dev(dz=NZ_RING - 1))
 
-    def halo_copy(j, source, side, sem, to):
+    def halo_copy(n, from_here, to, sem):
+        j, rows = n // 2, pl.ds(n % 2 * (ROWS // 2), ROWS // 2)
+        source = col_hbm.at[j, rows] if from_here else halo.at[1 - h, j, rows]
         return pltpu.make_async_remote_copy(
-            source, halo.at[side, j], h_s.at[sem], h_r.at[sem], device_id=to, device_id_type=MESH
+            source, halo.at[h, j, rows], h_s.at[sem], h_r.at[sem], device_id=to, device_id_type=MESH
         )
 
-    to_same = [halo_copy(j, col_hbm.at[j], h, j, same_z) for j in range(COLS)]
-    to_other = [halo_copy(j, col_hbm.at[j], 1 - h, 4 + j, other_z) for j in range(2)]
     beside = ((z + 1 - 2 * h + NZ_RING) % NZ_RING) * 2 + h, b
-    onward = [halo_copy(j, halo.at[1 - h, j], h, 4 + j, beside) for j in range(2, COLS)]
-    for copy in (to_same[2], to_same[3], to_other[0], to_same[0], to_other[1], to_same[1]):
+    to_same = [halo_copy(n, True, same_z, n) for n in range(2 * COLS)]
+    onward = [halo_copy(n, False, beside, 2 * COLS + n) for n in range(2 * COLS)]
+
+    def pass_on(first, last):
+        for n in range(first, last):
+            to_same[n].wait_recv()
+            onward[n].start()
+            if n + 4 < 2 * COLS:
+                to_same[n + 4].start()
+
+    for copy in to_same[:4]:
         copy.start()
 
     orbs = {}
@@ -143,10 +152,10 @@
             app[j, pl.ds(p * NY, NY), :] = total
         return carry
 
-    lax.fori_loop(0, COLS, local_terms, 0)
-    for copy, follower in zip(to_same[2:], onward):
-        copy.wait_recv()
-        follower.start()
+    lax.fori_loop(0, 2, local_terms, 0)
+    pass_on(0, 2)
+    lax.fori_loop(2, COLS, local_terms, 0)
+    pass_on(2, 8)
 
     def split(value):
         high = value.astype(jnp.bfloat16)
@@ -176,7 +185,6 @@
         return store
 
     orbs_y[2].start()
-    orbs_y[3].start()
     load_orb.wait()
     orbs[1].wait_recv()
     lay_out(phibuf, store_orbitals, 0, 4)
@@ -188,7 +196,7 @@
     signal(near_sem.at[2], dev(dz=2))
     signal(near_sem.at[3], dev(dz=NZ_RING - 2))
 
-    for copy in (*onward, *to_same[:2], *to_other):
+    for copy in onward:
         copy.wait_recv()
 
     def halo_terms(j, carry):
@@ -238,44 +246,61 @@
                 device_id=dev(dy=dy, dc=dc),
                 device_id_type=MESH,
             )
-    for dx in (2, 1, 3):
-        for dy in (0, 1):
-            block = acol.at[1, pl.ds(((yl + dy) % 2) * 32 + x * 8, 8)]
-            gathers[dx * 2 + dy] = pltpu.make_async_remote_copy(
-                block, block, gat_s.at[dx * 2 + dy], gat_r.at[dx * 2 + dy], device_id=dev(dx=dx), device_id_type=MESH
-            )
+    def block(dx, dy):
+        return acol.at[1, pl.ds(((yl + dy) % 2) * 32 + ((x + dx) % NX_RING) * 8, 8)]
+
+    def gather(n, at, dy, to):
+        return pltpu.make_async_remote_copy(
+            block(at, dy), block(at, dy), gat_s.at[n], gat_r.at[n], device_id=dev(dx=to), device_id_type=MESH
+        )
+
+    for dy in (0, 1):
+        gathers[1, dy] = gather(dy, 0, dy, 1)
+        gathers[3, dy] = gather(2 + dy, 0, dy, 3)
+    gathers[2, 0] = gather(4, 3, 0, 1)
+    gathers[2, 1] = gather(5, 1, 1, 3)
     for i in (6, 7, 2, 4, 3, 5, 1):
         cols[i].start()
     for i in (2, 3, 1):
         cols_y[i].start()
+    orbs_y[3].start()
     fwds[0].start()
     orbs[7].start()
+    for i in (2, 4, 3, 5):
+        orbs[i].wait_recv()
+    lay_out(phibuf, store_orbitals, 64, 8)
     own_col_y.wait()
     cols_y[1].wait_recv()
-    for dx in (2, 1, 3):
-        gathers[dx * 2].start()
+    for dx in (1, 3):
+        gathers[dx, 0].start()
     for i in (1, 2, 4, 3, 5):
         cols[i].wait_recv()
         fwds[i].start()
     for i in (2, 3):
         cols_y[i].wait_recv()
-    for dx in (2, 1, 3):
-        gathers[dx * 2 + 1].start()
+    for dx in (1, 3):
+        gathers[dx, 1].start()
+    gathers[1, 0].wait_recv()
+    gathers[2, 0].start()
     for i in (6, 7):
         cols[i].wait_recv()
         fwds[i].start()
-
-    for i in (2, 3, 4, 5, 6, 7):
-        orbs[i].wait_recv()
-    lay_out(phibuf, store_orbitals, 64, 12)
-    for i in (2, 3):
-        orbs_y[i].wait_recv()
-    lay_out(phibuf, store_orbitals, 320, 4)
+    gathers[3, 1].wait_recv()
+    gathers[2, 1].start()
 
     own_col.wait()
+    lay_out(acol.at[0], columns_to(0), yl * 32, 2)
+    orbs[6].wait_recv()
+    lay_out(phibuf, store_orbitals, 192, 2)
+    orbs_y[2].wait_recv()
+    lay_out(phibuf, store_orbitals, 320, 2)
+    orbs[7].wait_recv()
+    lay_out(phibuf, store_orbitals, 224, 2)
+    orbs_y[3].wait_recv()
+    lay_out(phibuf, store_orbitals, 352, 2)
     for i in range(8):
         fwds[i].wait_recv()
-    lay_out(acol.at[0], columns_to(0), 0, 4)
+    lay_out(acol.at[0], columns_to(0), 32 - yl * 32, 2)
 
     half_lanes = lax.broadcasted_iota(jnp.int32, (16, 128), 1) < 64
     dims = (((1,), (1,)), ((), ()))
@@ -321,8 +346,8 @@
     correlate(0, 0, 8)
     for i in (6, 7, 2, 4, 3, 5):
         send_parts(i)
-    for copy in gathers.values():
-        copy.wait_recv()
+    for n in ((3, 0), (1, 1), (2, 0), (2, 1)):
+        gathers[n].wait_recv()
     lay_out(acol.at[1], columns_to(1), 0, 4)
     correlate(1, 8, 4)
     for i in (10, 11, 1, 0):
@@ -406,12 +431,23 @@
             ry[k, side, q] = value
 
         removed(cts_y, last, side, to_x)
-    xs = {}
-    for dx in (2, 1, 3):
-        xs[dx] = pltpu.make_async_remote_copy(
-            ry.at[(x + dx) % NX_RING], ryin.at[dx], rx_s.at[dx], rx_r.at[dx], device_id=dev(dx=dx), device_id_type=MESH
+
+    def along_x(n, source, dx):
+        return pltpu.make_async_remote_copy(
+            source, ryin.at[n], rx_s.at[n], rx_r.at[n], device_id=dev(dx=dx), device_id_type=MESH
         )
-        xs[dx].start()
+
+    up, down = (x + 1) % NX_RING, (x + 3) % NX_RING
+    xs = {
+        0: along_x(0, ry.at[(x + 2) % NX_RING, 0], 1),
+        1: along_x(1, ry.at[(x + 2) % NX_RING, 1], 3),
+        2: along_x(2, ry.at[up, 1], 1),
+        3: along_x(3, ry.at[down, 0], 3),
+        4: along_x(4, rysum.at[0], 1),
+        5: along_x(5, rysum.at[1], 3),
+    }
+    for n in range(4):
+        xs[n].start()
     operands(corr[:256], cts)
     removed(cts, first, 1 - yl, to_send)
     order = (2, 1, 3, 0)
@@ -422,6 +458,10 @@
             rsend.at[k], rrecv.at[k], ry_s.at[dx], ry_r.at[dx], device_id=partner, device_id_type=MESH
         )
         ys[dx].start()
+    for n, to in ((0, up), (1, down)):
+        xs[n].wait_recv()
+        rysum[n] = ry[to, n] + ryin[n]
+        xs[4 + n].start()
     removed(cts, first, yl, to_own)
 
     own = corr[:32]
@@ -452,12 +492,10 @@
                     source, target, fin_s.at[n], fin_r.at[n], device_id=dev(dx=dx, dc=dc), device_id_type=MESH
                 )
                 fins[n].start()
-    value = ry[x]
-    for dx in (1, 3, 2):
-        xs[dx].wait_recv()
-        value = value + ryin[dx]
-    for side in (0, 1):
-        fin_y[side] = jnp.swapaxes(value[side], 0, 1)
+    for side, n, m in ((0, 3, 4), (1, 2, 5)):
+        xs[n].wait_recv()
+        xs[m].wait_recv()
+        fin_y[side] = jnp.swapaxes(ry[x, side] + ryin[n] + ryin[m], 0, 1)
     for i in (2, 3, 1, 0):
         dy, dc = STEPS_Y[i]
         source = fin_y.at[(yl + dy) % 2, pl.ds(((c + dc) % 2) * COLS, COLS)]
@@ -476,7 +514,7 @@
         copy.wait_recv()
     proj_ref[...] = app[...] - rem[...]
 
-    groups = [to_same, to_other, onward, zs, backs]
+    groups = [to_same, onward, zs, backs]
     groups += [g.values() for g in (orbs, orbs_y, cols, fwds, cols_y, gathers, sums, ys, xs, fins)]
     for group in groups:
         for copy in group:
@@ -506,13 +544,14 @@
         pltpu.VMEM((NX_RING, PART, 8, NX), f32),
         pltpu.VMEM((NX_RING, 8, PART, NX), f32),
         pltpu.VMEM((NX_RING, 2, PART, 8, NX), f32),
-        pltpu.VMEM((NX_RING, 2, PART, 8, NX), f32),
+        pltpu.VMEM((6, PART, 8, NX), f32),
+        pltpu.VMEM((2, PART, 8, NX), f32),
         pltpu.VMEM((2, 8, PART, NX), f32),
         pltpu.VMEM((COLS, ROWS, NX), f32),
         dma((8,)),
         pltpu.SemaphoreType.REGULAR((4,)),
         dma((8,)), dma((8,)),
-        dma((8,)), dma((8,)),
+        dma((16,)), dma((16,)),
         dma((8,)), dma((8,)),
         dma((8,)), dma((8,)),
         dma((4,)), dma((4,)),
@@ -523,7 +562,7 @@
         dma((20,)), dma((20,)),
         dma((4,)), dma((4,)),
         dma((8,)), dma((8,)),
-        dma((4,)), dma((4,)),
+        dma((6,)), dma((6,)),
         dma((4,)), dma((4,)),
     ]
     vmem, anywhere = pl.BlockSpec(memory_space=pltpu.VMEM), pl.BlockSpec(memory_space=pl.ANY)
@@ -537,13 +576,13 @@
         out_specs=(vmem, vmem),
         scratch_shapes=scratch,
         compiler_params=pltpu.CompilerParams(
-            collective_id=0, has_side_effects=True, vmem_limit_bytes=60 * 2**20
+            collective_id=0, has_side_effects=True, vmem_limit_bytes=40 * 2**20
         ),
         name="sternheimer",
     )(
-        columns.reshape(COLS, ROWS, NX),
-        potential.reshape(ROWS, NX),
-        orbitals.reshape(ORBS, ROWS, NX),
+        pltpu.with_memory_space_constraint(columns.reshape(COLS, ROWS, NX), pltpu.HBM),
+        pltpu.with_memory_space_constraint(potential.reshape(ROWS, NX), pltpu.HBM),
+        pltpu.with_memory_space_constraint(orbitals.reshape(ORBS, ROWS, NX), pltpu.HBM),
     )
     return projected.reshape(columns.shape), correlation
 

time: 77.1 us -> 73.7 us (0.956)
  local copies, waits for them, and re-layouts: 3.09 us -> 1.35 us
  Pallas kernels: 73.2 us -> 71.6 us
    unnamed x2, local copies, waits for them, and re-layouts: 3.09 us -> 1.35 us
    pallas_call x1, Pallas kernels: 73.2 us -> 71.6 us  [shards(): pl.pallas_call(kernel, out_shape=(jax.ShapeDtypeStruct((COLS, ROWS, NX),...]
where the time goes in v5:
time: 73.7 us; the launch traced here: 73.6 us
  Pallas kernels  71.6 us (97%)
  local copies, waits for them, and re-layouts  1.35 us (2%)
    pallas_call x1, Pallas kernels, shards(): pl.pallas_call(kernel, out_shape=(jax.ShapeDtypeStruct((COLS, ROWS, NX),...  71.6 us

profile of v5, /device:TPU:1, one launch (start us, length us, event | category | flops | bytes accessed | tf_op | source)
XLA Modules:
  0.0 73.6 jit_solution(10066786102236512425)
XLA Ops:
  0.6 71.6 %sternheimer.1 = (f32[4,192,128]{2,1,0:T(8,128)S(1)}, f32[32,64]{1,0:T(8,128)S(1)}) custom-call(f32[4,192,128]{2,1,0:T(8,128)} %bitcast.6, f32[192,128]{1,0:T(8,128)} %bitcast.7, f32[32,192,128]{2,1,0:T(8,128)} %bitcast.5), custom_call_target="tpu_custom_call" | custom-call | tf_op jit(solution)/shard_map/sternheimer/pallas_call | solution.py:569
  72.2 0.7 %copy.7 = f32[4,6,32,128]{3,2,1,0:T(8,128)} copy(f32[4,6,32,128]{3,2,1,0:T(8,128)S(1)} %bitcast.4) | data formatting | bytes 786432
  73.0 0.6 copy.8

commit v6 on v5

--- a/solution.py
+++ b/solution.py
@@ -30,7 +30,7 @@
 def kernel(
     col_hbm, pot_hbm, orb_hbm, proj_ref, corr_ref,
     colv, potv, halo, app, phibuf, phi, acol, ahl, cpart, cin, zin, ctot, cts, cts_y,
-    rsend, rrecv, rown, fin, ry, ryin, rysum, fin_y, rem,
+    rx, rrecv, fin, ry, ryin, rysum, fin_y, rem,
     loc_sem, near_sem, orb_s, orb_r, h_s, h_r, col_s, col_r, fwd_s, fwd_r,
     orby_s, orby_r, coly_s, coly_r, gat_s, gat_r,
     s1_s, s1_r, s2_s, s2_r, s3_s, s3_r, ry_s, ry_r, fin_s, fin_r, rx_s, rx_r, finy_s, finy_r,
@@ -172,10 +172,16 @@
 
         lax.fori_loop(0, blocks, one, 0)
 
-    def store_orbitals(row, at, high, low):
-        rows = pl.ds(pl.multiple_of(row, 16), 16)
-        phi[0, rows, at] = high
-        phi[1, rows, at] = low
+    def orbitals_to(base, n):
+        def store(row, at, high, low):
+            k = (row - base) // 16
+            rows = pl.ds(pl.multiple_of(base + k % 2 * (n * 16) + k // 2 * 16, 16), 16)
+            phi[0, rows, at] = high
+            phi[1, rows, at] = low
+
+        return store
+
+    first_rows, last_rows = orbitals_to(0, 8), orbitals_to(256, 4)
 
     def columns_to(mode):
         def store(row, at, high, low):
@@ -187,10 +193,10 @@
     orbs_y[2].start()
     load_orb.wait()
     orbs[1].wait_recv()
-    lay_out(phibuf, store_orbitals, 0, 4)
+    lay_out(phibuf, first_rows, 0, 4)
     load_orb_y.wait()
     orbs_y[1].wait_recv()
-    lay_out(phibuf, store_orbitals, 256, 4)
+    lay_out(phibuf, last_rows, 256, 4)
     for i in (0, 1):
         pl.semaphore_wait(near_sem.at[i], 1)
     signal(near_sem.at[2], dev(dz=2))
@@ -259,16 +265,15 @@
         gathers[3, dy] = gather(2 + dy, 0, dy, 3)
     gathers[2, 0] = gather(4, 3, 0, 1)
     gathers[2, 1] = gather(5, 1, 1, 3)
-    for i in (6, 7, 2, 4, 3, 5, 1):
+    for i in (1, 2, 4, 3, 5, 6, 7):
         cols[i].start()
     for i in (2, 3, 1):
         cols_y[i].start()
     orbs_y[3].start()
     fwds[0].start()
-    orbs[7].start()
     for i in (2, 4, 3, 5):
         orbs[i].wait_recv()
-    lay_out(phibuf, store_orbitals, 64, 8)
+    lay_out(phibuf, first_rows, 64, 8)
     own_col_y.wait()
     cols_y[1].wait_recv()
     for dx in (1, 3):
@@ -280,6 +285,7 @@
         cols_y[i].wait_recv()
     for dx in (1, 3):
         gathers[dx, 1].start()
+    orbs[7].start()
     gathers[1, 0].wait_recv()
     gathers[2, 0].start()
     for i in (6, 7):
@@ -291,13 +297,13 @@
     own_col.wait()
     lay_out(acol.at[0], columns_to(0), yl * 32, 2)
     orbs[6].wait_recv()
-    lay_out(phibuf, store_orbitals, 192, 2)
+    lay_out(phibuf, first_rows, 192, 2)
     orbs_y[2].wait_recv()
-    lay_out(phibuf, store_orbitals, 320, 2)
+    lay_out(phibuf, last_rows, 320, 2)
     orbs[7].wait_recv()
-    lay_out(phibuf, store_orbitals, 224, 2)
+    lay_out(phibuf, first_rows, 224, 2)
     orbs_y[3].wait_recv()
-    lay_out(phibuf, store_orbitals, 352, 2)
+    lay_out(phibuf, last_rows, 352, 2)
     for i in range(8):
         fwds[i].wait_recv()
     lay_out(acol.at[0], columns_to(0), 32 - yl * 32, 2)
@@ -311,8 +317,8 @@
         low = lax.dot_general(phi[1, rows, :], ahl[mode], dims, preferred_element_type=jnp.float32)
         value = high + pltpu.roll(high, 64, 1) + low
         for i in range(n):
-            first = value[i * ORBS : i * ORBS + 16]
-            second = value[i * ORBS + 16 : i * ORBS + 32]
+            first = value[i * 16 : i * 16 + 16]
+            second = value[(n + i) * 16 : (n + i) * 16 + 16]
             packed = jnp.where(half_lanes, first, pltpu.roll(second, 64, 1))
             if i0 + i in (8, 9):
                 cpart[i0 + i - 8, 0] += packed[:8]
@@ -396,41 +402,28 @@
     for copy in backs:
         copy.wait_recv()
 
-    packed = ctot[...].reshape(10, 16, 128)
-    swapped = pltpu.roll(packed.reshape(160, 128), 64, 1).reshape(10, 16, 128)
-    corr = jnp.concatenate([packed, swapped], axis=1).reshape(320, 128)
-    corr_y = jnp.concatenate([corr[:64], corr[256:]], axis=0)
-
-    def operands(value, out):
-        high, low = split(jnp.transpose(value)[:64])
-        for side in (0, 1):
-            out[side, pl.ds(0, 32), :] = high[side * 32 : side * 32 + 32]
-            out[side, pl.ds(32, 32), :] = low[side * 32 : side * 32 + 32]
-
-    def removed(left, rows, side, out):
+    def operand(packed, out):
+        high, low = split(packed)
+        out[pl.ds(0, 64), :] = high
+        out[pl.ds(64, 64), :] = low
+
+    def removed(left, rows, out):
         for q0 in range(0, PART, 4):
             at = pl.ds(q0 * NX, 4 * NX)
-            both = jnp.dot(left[side], phi[0, rows, at], preferred_element_type=jnp.float32)
-            rest = jnp.dot(left[side, pl.ds(0, 32), :], phi[1, rows, at], preferred_element_type=jnp.float32)
-            value = both[:32] + both[32:] + rest
+            both = jnp.dot(left[...], phi[0, rows, at], preferred_element_type=jnp.float32)
+            rest = jnp.dot(left[pl.ds(0, 64), :], phi[1, rows, at], preferred_element_type=jnp.float32)
+            value = both[:64] + both[64:] + rest
             for q in range(4):
-                for k in range(NX_RING):
-                    out(k, q0 + q, value[k * 8 : k * 8 + 8, q * NX : (q + 1) * NX])
-
-    def to_send(k, q, value):
-        rsend[k, q] = value
-
-    def to_own(k, q, value):
-        rown[k, q] = value
-
-    first, last = pl.ds(0, 256), pl.ds(256, 128)
-    operands(corr_y, cts_y)
-    for side in (0, 1):
-
-        def to_x(k, q, value):
-            ry[k, side, q] = value
-
-        removed(cts_y, last, side, to_x)
+                for side in (0, 1):
+                    for k in range(NX_RING):
+                        n = side * 32 + k * 8
+                        out[side, k, q0 + q] = value[n : n + 8, q * NX : (q + 1) * NX]
+
+    packed = jnp.concatenate([ctot[0:2].reshape(32, 128), ctot[8:10].reshape(32, 128)], axis=0)
+    turned = jnp.transpose(jnp.concatenate([packed, packed], axis=0))
+    low_lanes = lax.broadcasted_iota(jnp.int32, (64, 128), 1) < 64
+    operand(jnp.where(low_lanes, turned[:64], turned[64:]), cts_y)
+    removed(cts_y, pl.ds(256, 128), ry)
 
     def along_x(n, source, dx):
         return pltpu.make_async_remote_copy(
@@ -439,32 +432,34 @@
 
     up, down = (x + 1) % NX_RING, (x + 3) % NX_RING
     xs = {
-        0: along_x(0, ry.at[(x + 2) % NX_RING, 0], 1),
-        1: along_x(1, ry.at[(x + 2) % NX_RING, 1], 3),
-        2: along_x(2, ry.at[up, 1], 1),
-        3: along_x(3, ry.at[down, 0], 3),
+        0: along_x(0, ry.at[0, (x + 2) % NX_RING], 1),
+        1: along_x(1, ry.at[1, (x + 2) % NX_RING], 3),
+        2: along_x(2, ry.at[1, up], 1),
+        3: along_x(3, ry.at[0, down], 3),
         4: along_x(4, rysum.at[0], 1),
         5: along_x(5, rysum.at[1], 3),
     }
     for n in range(4):
         xs[n].start()
-    operands(corr[:256], cts)
-    removed(cts, first, 1 - yl, to_send)
+
+    turned = jnp.transpose(ctot[0:8].reshape(128, 128))
+    operand(jnp.concatenate([turned[:64], turned[64:]], axis=1), cts)
+    removed(cts, pl.ds(0, 256), rx)
     order = (2, 1, 3, 0)
     ys = {}
     for dx in order:
         k = (x + dx) % NX_RING
         ys[dx] = pltpu.make_async_remote_copy(
-            rsend.at[k], rrecv.at[k], ry_s.at[dx], ry_r.at[dx], device_id=partner, device_id_type=MESH
+            rx.at[1 - yl, k], rrecv.at[k], ry_s.at[dx], ry_r.at[dx], device_id=partner, device_id_type=MESH
         )
         ys[dx].start()
     for n, to in ((0, up), (1, down)):
         xs[n].wait_recv()
-        rysum[n] = ry[to, n] + ryin[n]
+        rysum[n] = ry[n, to] + ryin[n]
         xs[4 + n].start()
-    removed(cts, first, yl, to_own)
-
-    own = corr[:32]
+
+    packed = ctot[0].reshape(16, 128)
+    own = jnp.concatenate([packed, pltpu.roll(packed, 64, 1)], axis=0)
     lane = lax.broadcasted_iota(jnp.int32, (ORBS, 128), 1)
     value = own
     for side in (0, 1):
@@ -476,40 +471,43 @@
     corr_ref[...] = value[:, :64]
 
     fins = {}
-    for dx in order:
+
+    def finish(dx):
         k = (x + dx) % NX_RING
         ys[dx].wait_recv()
-        fin[k] = jnp.swapaxes(rown[k] + rrecv[k], 0, 1)
+        fin[k] = jnp.swapaxes(rx[yl, k] + rrecv[k], 0, 1)
         for dc in (1, 0):
             source = fin.at[k, pl.ds(((c + dc) % 2) * COLS, COLS)]
             target = rem.at[:, rows_of(me), :]
             n = STEPS.index((dx, dc))
             if n == 0:
-                local = pltpu.make_async_copy(source, target, loc_sem.at[3])
-                local.start()
+                fins[n] = pltpu.make_async_copy(source, target, loc_sem.at[3])
             else:
                 fins[n] = pltpu.make_async_remote_copy(
                     source, target, fin_s.at[n], fin_r.at[n], device_id=dev(dx=dx, dc=dc), device_id_type=MESH
                 )
-                fins[n].start()
+            fins[n].start()
+
+    for dx in order[:3]:
+        finish(dx)
     for side, n, m in ((0, 3, 4), (1, 2, 5)):
         xs[n].wait_recv()
         xs[m].wait_recv()
-        fin_y[side] = jnp.swapaxes(ry[x, side] + ryin[n] + ryin[m], 0, 1)
+        fin_y[side] = jnp.swapaxes(ry[side, x] + ryin[n] + ryin[m], 0, 1)
     for i in (2, 3, 1, 0):
         dy, dc = STEPS_Y[i]
         source = fin_y.at[(yl + dy) % 2, pl.ds(((c + dc) % 2) * COLS, COLS)]
         target = rem.at[:, rows_y(0, 0), :]
         if i == 0:
-            local_y = pltpu.make_async_copy(source, target, loc_sem.at[7])
-            local_y.start()
+            fins[8] = pltpu.make_async_copy(source, target, loc_sem.at[7])
         else:
             fins[8 + i] = pltpu.make_async_remote_copy(
                 source, target, finy_s.at[i], finy_r.at[i], device_id=dev(dy=dy, dc=dc), device_id_type=MESH
             )
-            fins[8 + i].start()
-    local.wait()
-    local_y.wait()
+        fins[8 + i].start()
+    finish(0)
+    fins.pop(0).wait()
+    fins.pop(8).wait()
     for copy in fins.values():
         copy.wait_recv()
     proj_ref[...] = app[...] - rem[...]
@@ -537,13 +535,12 @@
         pltpu.VMEM((20, 8, 128), f32),
         pltpu.VMEM((NZ_RING, 8, 128), f32),
         pltpu.VMEM((10, 2, 8, 128), f32),
-        pltpu.VMEM((2, 64, 256), bf16),
-        pltpu.VMEM((2, 64, 128), bf16),
-        pltpu.VMEM((NX_RING, PART, 8, NX), f32),
-        pltpu.VMEM((NX_RING, PART, 8, NX), f32),
+        pltpu.VMEM((128, 256), bf16),
+        pltpu.VMEM((128, 128), bf16),
+        pltpu.VMEM((2, NX_RING, PART, 8, NX), f32),
         pltpu.VMEM((NX_RING, PART, 8, NX), f32),
         pltpu.VMEM((NX_RING, 8, PART, NX), f32),
-        pltpu.VMEM((NX_RING, 2, PART, 8, NX), f32),
+        pltpu.VMEM((2, NX_RING, PART, 8, NX), f32),
         pltpu.VMEM((6, PART, 8, NX), f32),
         pltpu.VMEM((2, PART, 8, NX), f32),
         pltpu.VMEM((2, 8, PART, NX), f32),

time: 73.7 us -> 72.1 us (0.978)
  Pallas kernels: 71.6 us -> 70.1 us
    pallas_call x1, Pallas kernels: 71.6 us -> 70.1 us  [shards(): pl.pallas_call(kernel, out_shape=(jax.ShapeDtypeStruct((COLS, ROWS, NX),...]
where the time goes in v6:
time: 72.1 us; the launch traced here: 72 us
  Pallas kernels  70.1 us (97%)
  local copies, waits for them, and re-layouts  1.35 us (2%)
    pallas_call x1, Pallas kernels, shards(): pl.pallas_call(kernel, out_shape=(jax.ShapeDtypeStruct((COLS, ROWS, NX),...  70.1 us

profile of v6, /device:TPU:1, one launch (start us, length us, event | category | flops | bytes accessed | tf_op | source)
XLA Modules:
  0.0 72.0 jit_solution(9713531429673124509)
XLA Ops:
  0.6 70.1 %sternheimer.1 = (f32[4,192,128]{2,1,0:T(8,128)S(1)}, f32[32,64]{1,0:T(8,128)S(1)}) custom-call(f32[4,192,128]{2,1,0:T(8,128)} %bitcast.6, f32[192,128]{1,0:T(8,128)} %bitcast.7, f32[32,192,128]{2,1,0:T(8,128)} %bitcast.5), custom_call_target="tpu_custom_call" | custom-call | tf_op jit(solution)/shard_map/sternheimer/pallas_call | solution.py:566
  70.7 0.7 %copy.7 = f32[4,6,32,128]{3,2,1,0:T(8,128)} copy(f32[4,6,32,128]{3,2,1,0:T(8,128)S(1)} %bitcast.4) | data formatting | bytes 786432
  71.4 0.6 copy.8

commit v7 on v6

--- a/solution.py
+++ b/solution.py
@@ -352,9 +352,12 @@
     correlate(0, 0, 8)
     for i in (6, 7, 2, 4, 3, 5):
         send_parts(i)
-    for n in ((3, 0), (1, 1), (2, 0), (2, 1)):
+    for n in ((3, 0), (2, 0)):
         gathers[n].wait_recv()
-    lay_out(acol.at[1], columns_to(1), 0, 4)
+    lay_out(acol.at[1], columns_to(1), yl * 32, 2)
+    for n in ((1, 1), (2, 1)):
+        gathers[n].wait_recv()
+    lay_out(acol.at[1], columns_to(1), 32 - yl * 32, 2)
     correlate(1, 8, 4)
     for i in (10, 11, 1, 0):
         send_parts(i)

time: 72.1 us -> 72.1 us (level)
  no operation moved by 1% of the time
where the time goes in v7:
time: 72.1 us
  Pallas kernels  70.1 us (97%)
  local copies, waits for them, and re-layouts  1.35 us (2%)
    pallas_call x1, Pallas kernels, shards(): pl.pallas_call(kernel, out_shape=(jax.ShapeDtypeStruct((COLS, ROWS, NX),...  70.1 us

profile of v7, /device:TPU:1, one launch (start us, length us, event | category | flops | bytes accessed | tf_op | source)
XLA Modules:
  0.0 72.1 jit_solution(12939214503154459367)
XLA Ops:
  0.6 70.1 %sternheimer.1 = (f32[4,192,128]{2,1,0:T(8,128)S(1)}, f32[32,64]{1,0:T(8,128)S(1)}) custom-call(f32[4,192,128]{2,1,0:T(8,128)} %bitcast.6, f32[192,128]{1,0:T(8,128)} %bitcast.7, f32[32,192,128]{2,1,0:T(8,128)} %bitcast.5), custom_call_target="tpu_custom_call" | custom-call | tf_op jit(solution)/shard_map/sternheimer/pallas_call | solution.py:569
  70.7 0.7 %copy.7 = f32[4,6,32,128]{3,2,1,0:T(8,128)} copy(f32[4,6,32,128]{3,2,1,0:T(8,128)S(1)} %bitcast.4) | data formatting | bytes 786432
  71.4 0.6 copy.8
